TPU v7x, 32 devices: a whole 2x2x4 slice. The times are simulated.
32 devices in a mesh: file: 2 (over x), seq: 4 (over z), tp: 4 (over y, core).
Axes of the slice: x: 2, y: 2, z: 4, core: 2. Of those that a mesh axis runs over, the one named last changes fastest.
Arguments:
- queries: bfloat16 [4096, 4096], P(('file', 'tp', 'seq')), parts along dimension 0
- keys: bfloat16 [4096, 1024], P(('file', 'tp', 'seq')), parts along dimension 0
- values: bfloat16 [4096, 1024], P(('file', 'tp', 'seq')), parts along dimension 0, may hold values from -6 to 6
- mem_pos: int32 [256], P(('file', 'tp', 'seq')), parts along dimension 0, may hold values from 0 to 2047, as said below
- norm_gain: float32 [4096], replicated, may hold values from 0.1 to 1.9
- summary_weight: bfloat16 [4096, 6144], P('tp', 'seq'), may hold values from -0.09375 to 0.09375
Outputs:
- encoded: bfloat16 [4096, 4096], P(('file', 'tp', 'seq')), parts along dimension 0
- summary: bfloat16 [256, 6144], P(('file', 'tp'), 'seq'), parts along dimension 0
There are 2 independent parts, one for each index of `file`. A program takes and returns all parts, laid end to end along the dimension named above; an argument that names none is the same for every part. Nothing has to cross between parts.
Inputs may be any that keep to these rules, and one draw needn't show every extreme that they name: `mem_pos`: entry j lies among rows 16 * j to 16 * j + 15.
All inputs are finite; a program needn't handle non-finite values.
Results may differ from a plain program's by a relative error of at most 0.018.
Values may be sent and summed in bfloat16 or wider, within the bound.
A program may use at most 64 MiB of HBM per device.

v0:
```python
import jax
import jax.numpy as jnp
from jax import lax
from jax.sharding import PartitionSpec as P

D = 4096
HEADS = 32
KV_HEADS = 8
HEAD_DIM = 128


def from_behind(block, axis, distance):
    devices = range(lax.axis_size(axis))
    route = [(i - distance, i) for i in devices if i - distance in devices]
    return lax.ppermute(block, axis, route)


def widen(packed):
    count = packed.shape[0]
    group = HEADS // KV_HEADS
    spread = jnp.broadcast_to(
        packed.reshape(count, KV_HEADS, 1, HEAD_DIM), (count, KV_HEADS, group, HEAD_DIM)
    )
    return spread.reshape(count, HEADS * HEAD_DIM)


def on_device(queries, keys, values, mem_pos, norm_gain, summary_weight):
    rows = queries.shape[0]
    n_seq = lax.axis_size("seq")
    n_tp = lax.axis_size("tp")
    heads_dev = HEADS // n_seq
    scale = 1.0 / HEAD_DIM**0.5
    span = rows * n_seq
    block = 512
    blocks = span // block
    shifted = from_behind(jnp.stack((keys, values)), "tp", 1)
    moved_q, moved_k, moved_v, prior_k, prior_v = (
        lax.all_to_all(queries, "seq", split_axis=1, concat_axis=0, tiled=True),
        lax.all_to_all(widen(keys), "seq", split_axis=1, concat_axis=0, tiled=True),
        lax.all_to_all(widen(values), "seq", split_axis=1, concat_axis=0, tiled=True),
        lax.all_to_all(widen(shifted[0]), "seq", split_axis=1, concat_axis=0, tiled=True),
        lax.all_to_all(widen(shifted[1]), "seq", split_axis=1, concat_axis=0, tiled=True),
    )
    query_heads = moved_q.reshape(span, heads_dev, HEAD_DIM)
    keys_all = jnp.concatenate((prior_k, moved_k), axis=0)
    values_all = jnp.concatenate((prior_v, moved_v), axis=0)
    has_prior = lax.axis_index("tp") > 0

    def one_block(qb):
        q_first = qb * block
        q_block = lax.dynamic_slice_in_dim(query_heads, q_first, block, 0)
        q_where = q_first + jnp.arange(block, dtype=jnp.int32)

        def step(index, state):
            peak, total, accum = state
            k_first = q_first + index * block
            key_block = lax.dynamic_slice_in_dim(keys_all, k_first, block, 0).reshape(
                block, heads_dev, HEAD_DIM
            )
            value_block = lax.dynamic_slice_in_dim(values_all, k_first, block, 0).reshape(
                block, heads_dev, HEAD_DIM
            )
            k_where = k_first + jnp.arange(block, dtype=jnp.int32)
            seen = (k_where[None, :] > q_where[:, None]) & (
                k_where[None, :] <= q_where[:, None] + span
            )
            seen = seen & ((k_where >= span) | has_prior)[None, :]
            scores = (
                jnp.einsum("qhd,khd->qhk", q_block, key_block, preferred_element_type=jnp.float32)
                * scale
            )
            masked = jnp.where(seen[:, None, :], scores, -jnp.inf)
            newest = jnp.maximum(peak, jnp.max(masked, axis=2))
            fade = jnp.exp(peak - newest)
            weights = jnp.where(seen[:, None, :], jnp.exp(scores - newest[:, :, None]), 0.0)
            total = total * fade + jnp.sum(weights, axis=2)
            accum = accum * fade[:, :, None] + jnp.einsum(
                "qhk,khd->qhd",
                weights.astype(jnp.bfloat16),
                value_block,
                preferred_element_type=jnp.float32,
            )
            return (newest, total, accum)

        start_state = (
            jnp.full((block, heads_dev), -1e30, jnp.float32),
            jnp.zeros((block, heads_dev), jnp.float32),
            jnp.zeros((block, heads_dev, HEAD_DIM), jnp.float32),
        )
        peak, total, accum = lax.fori_loop(0, blocks + 1, step, start_state)
        return accum / total[:, :, None]

    pieces = lax.map(one_block, jnp.arange(blocks, dtype=jnp.int32))
    attended = pieces.reshape(span, heads_dev * HEAD_DIM).astype(jnp.bfloat16)
    encoded = lax.all_to_all(attended, "seq", split_axis=0, concat_axis=1, tiled=True)
    local_rows = mem_pos % rows
    picked = jnp.take(encoded, local_rows, axis=0).astype(jnp.float32)
    meansq = jnp.mean(picked * picked, axis=1, keepdims=True)
    normed = (picked * lax.rsqrt(meansq + 1e-05) * norm_gain[None, :]).astype(jnp.bfloat16)
    mem_dev = normed.shape[0]
    width = D // n_tp
    memory_full = lax.all_gather(normed, ("seq", "tp"), axis=0, tiled=True)
    ordered = jnp.transpose(memory_full.reshape(n_seq, n_tp, mem_dev, D), (1, 0, 2, 3)).reshape(
        n_tp * n_seq * mem_dev, D
    )
    memory_mine = lax.dynamic_slice_in_dim(ordered, lax.axis_index("tp") * width, width, 1)
    summary = lax.psum_scatter(
        jnp.dot(memory_mine, summary_weight, preferred_element_type=jnp.float32).astype(
            jnp.bfloat16
        ),
        "tp",
        scatter_dimension=0,
        tiled=True,
    )
    return (encoded, summary)


def solution(mesh):
    placed = (
        P(("file", "tp", "seq"), None),
        P(("file", "tp", "seq"), None),
        P(("file", "tp", "seq"), None),
        P(("file", "tp", "seq")),
        P(),
        P("tp", "seq"),
    )
    return jax.shard_map(
        on_device,
        mesh=mesh,
        in_specs=placed,
        out_specs=(P(("file", "tp", "seq"), None), P(("file", "tp"), "seq")),
        check_vma=False,
    )
```

profile of v0, /device:TPU:0, one launch (start us, length us, event | category | flops | bytes accessed | tf_op | source)
XLA Modules:
  0.0 333.6 jit_solution(5630359536273569941)
XLA Ops:
  9.7 6.3 %all-to-all-start.4 = ((bf16[128,4,1024]{0,2,1:T(8,128)(2,1)}), bf16[128,4,1024]{0,2,1:T(8,128)(2,1)}, u32[]{:S(2)}, u32[]{:S(2)}) async-start(bf16[128,4,1024]{0,2,1:T(8,128)(2,1)} %bitcast.81), calls=%async_computation.4 | async-start | bytes 2097152 | tf_op jit(solution)/shard_map/all_to_all | solution.py:40
  17.1 24.7 %all-to-all-done.4 = bf16[128,4,1024]{0,2,1:T(8,128)(2,1)} async-done(((bf16[128,4,1024]{0,2,1:T(8,128)(2,1)}), bf16[128,4,1024]{0,2,1:T(8,128)(2,1)}, u32[]{:S(2)}, u32[]{:S(2)}) %all-to-all-start.4) | async-done | bytes 1048608 | tf_op jit(solution)/shard_map/all_to_all | solution.py:40
  43.0 4.4 %all-to-all-start.1 = ((bf16[128,4,1024]{0,2,1:T(8,128)(2,1)}), bf16[128,4,1024]{0,2,1:T(8,128)(2,1)}, u32[]{:S(2)}, u32[]{:S(2)}) async-start(bf16[128,4,1024]{0,2,1:T(8,128)(2,1)} %bitcast.82), calls=%async_computation.1 | async-start | bytes 2097152 | tf_op jit(solution)/shard_map/all_to_all | solution.py:39
  49.7 23.0 %all-to-all-done.1 = bf16[128,4,1024]{0,2,1:T(8,128)(2,1)} async-done(((bf16[128,4,1024]{0,2,1:T(8,128)(2,1)}), bf16[128,4,1024]{0,2,1:T(8,128)(2,1)}, u32[]{:S(2)}, u32[]{:S(2)}) %all-to-all-start.1) | async-done | bytes 1048608 | tf_op jit(solution)/shard_map/all_to_all | solution.py:39
  72.7 4.2 %all-to-all-start.2 = ((bf16[128,4,1024]{2,0,1:T(8,128)(2,1)}), bf16[128,4,1024]{2,0,1:T(8,128)(2,1)}, u32[]{:S(2)}, u32[]{:S(2)}) async-start(bf16[128,4,1024]{2,0,1:T(8,128)(2,1)} %bitcast.83), calls=%async_computation.2 | async-start | bytes 2097152 | tf_op jit(solution)/shard_map/all_to_all | solution.py:38
  82.8 19.5 %all-to-all-done.2 = bf16[128,4,1024]{2,0,1:T(8,128)(2,1)} async-done(((bf16[128,4,1024]{2,0,1:T(8,128)(2,1)}), bf16[128,4,1024]{2,0,1:T(8,128)(2,1)}, u32[]{:S(2)}, u32[]{:S(2)}) %all-to-all-start.2) | async-done | bytes 1048608 | tf_op jit(solution)/shard_map/all_to_all | solution.py:38
  103.4 4.3 %all-to-all-start.3 = ((bf16[128,4,1024]{0,2,1:T(8,128)(2,1)}), bf16[128,4,1024]{0,2,1:T(8,128)(2,1)}, u32[]{:S(2)}, u32[]{:S(2)}) async-start(bf16[128,4,1024]{0,2,1:T(8,128)(2,1)} %bitcast.80), calls=%async_computation.3 | async-start | bytes 2097152 | tf_op jit(solution)/shard_map/all_to_all | solution.py:42
  108.8 24.1 %all-to-all-done.3 = bf16[128,4,1024]{0,2,1:T(8,128)(2,1)} async-done(((bf16[128,4,1024]{0,2,1:T(8,128)(2,1)}), bf16[128,4,1024]{0,2,1:T(8,128)(2,1)}, u32[]{:S(2)}, u32[]{:S(2)}) %all-to-all-start.3) | async-done | bytes 1048608 | tf_op jit(solution)/shard_map/all_to_all | solution.py:42
  134.2 4.2 %all-to-all-start = ((bf16[128,4,1024]{0,2,1:T(8,128)(2,1)}), bf16[128,4,1024]{0,2,1:T(8,128)(2,1)}, u32[]{:S(2)}, u32[]{:S(2)}) async-start(bf16[128,4,1024]{0,2,1:T(8,128)(2,1)} %bitcast.79), calls=%async_computation | async-start | bytes 2097152 | tf_op jit(solution)/shard_map/all_to_all | solution.py:41
  148.0 15.8 %all-to-all-done = bf16[128,4,1024]{0,2,1:T(8,128)(2,1)} async-done(((bf16[128,4,1024]{0,2,1:T(8,128)(2,1)}), bf16[128,4,1024]{0,2,1:T(8,128)(2,1)}, u32[]{:S(2)}, u32[]{:S(2)}) %all-to-all-start) | async-done | bytes 1048608 | tf_op jit(solution)/shard_map/all_to_all | solution.py:41
  166.0 4.6 %pad_maximum_fusion = (bf16[1024,1024]{1,0:T(8,128)(2,1)}, bf16[1024,1024]{1,0:T(8,128)(2,1)}) fusion(bf16[512,1024]{1,0:T(8,128)(2,1)} %bitcast.86, bf16[512,1024]{1,0:T(8,128)(2,1)} %bitcast.88, bf16[512,1024]{1,0:T(8,128)(2,1)} %bitcast.85, bf16[512,1024]{1,0:T(8,128)(2,1)} %bitcast.87), kind=kLoop, calls=%fused_computation.31 | loop fusion | flops 8388608 | bytes 8388608 | tf_op jit(solution)/shard_map/concatenate | solution.py:45
  170.6 53.9 %while.28 = (s32[]{:T(128)}, f32[512,8]{0,1:T(8,128)S(1)}, f32[512,8]{0,1:T(8,128)S(1)}, f32[512,8,128]{0,2,1:T(8,128)}, pred[]{:T(512)}, /*index=5*/bf16[1024,1...) while((s32[]{:T(128)}, f32[512,8]{0,1:T(8,128)S(1)}, ...), condition=%wide.region_3.0_spmd.clone.clone, body=%wide.region_0.3_spmd.clone.clone.sunk | while | flops 1099454976 | bytes 42214584 | solution.py:90
  170.9 3.0 constant_dynamic-slice_fusion.3
  176.3 6.4 %fusion.44 = (f32[512,8]{0,1:T(8,128)S(1)}, f32[8,512,512]{2,1,0:T(8,128)}) fusion(pred[512,512]{0,1:T(8,128)(4,1)S(1)} %fusion.43, bf16[512,8,128]{0,2,1:T(8,128)(2,1)} %bitcast.77, bf16[512,8,128]{2,0,1:T(8,128)(2,1)} %get-tuple-element.434), kind=kOutput, calls=%fused_computation.4.clone.1 | convolution fusion | flops 543158272 | bytes 10764288 | tf_op jit(solution)/shard_map/while/body/eval_jaxpr/while/body/eval_jaxpr/qhd,khd->qhk/dot_general | solution.py:69
  182.7 5.1 %fusion.45 = f32[512,8]{0,1:T(8,128)S(1)} fusion(f32[8,512,512]{2,1,0:T(8,128)} %get-tuple-element.400, f32[512,8]{0,1:T(8,128)S(1)} %select_maximum_fusion.2, pred[512,512]{0,1:T(8,128)(4,1)S(1)} %fusion.43), kind=kLoop, calls=%fused_computation.8.clone.1 | loop fusion | flops 8384512 | bytes 8683520 | tf_op jit(solution)/shard_map/while/body/eval_jaxpr/while/body/eval_jaxpr/reduce_sum | solution.py:76
  190.1 7.1 %bitcast_add_fusion.2 = f32[512,8,128]{0,2,1:T(8,128)} fusion(f32[512,8,128]{0,2,1:T(8,128)} %get-tuple-element.419, bf16[512,8,128]{0,2,1:T(8,128)(2,1)} %bitcast.78, f32[8,512,512]{2,1,0:T(8,128)} %get-tuple-element.400, f32[512,8]{0,1:T(8,128)S(1)} %select_maximum_fusion.2, pred[512,512]{0,1:T(8,128)(4,1)S(1)} %fusion.43, ...), kind=kOutput, calls=%fused_computation.14.clone.1 | convolution fusion | flops 546832384 | bytes 13926401 | tf_op jit(solution)/shard_map/while/body/eval_jaxpr/while/body/eval_jaxpr/qhk,khd->qhd/dot_general | solution.py:77
  197.6 3.0 constant_dynamic-slice_fusion.3
  202.9 6.4 %fusion.44 = (f32[512,8]{0,1:T(8,128)S(1)}, f32[8,512,512]{2,1,0:T(8,128)}) fusion(pred[512,512]{0,1:T(8,128)(4,1)S(1)} %fusion.43, bf16[512,8,128]{0,2,1:T(8,128)(2,1)} %bitcast.77, bf16[512,8,128]{2,0,1:T(8,128)(2,1)} %get-tuple-element.434), kind=kOutput, calls=%fused_computation.4.clone.1 | convolution fusion | flops 543158272 | bytes 10764288 | tf_op jit(solution)/shard_map/while/body/eval_jaxpr/while/body/eval_jaxpr/qhd,khd->qhk/dot_general | solution.py:69
  209.3 5.1 %fusion.45 = f32[512,8]{0,1:T(8,128)S(1)} fusion(f32[8,512,512]{2,1,0:T(8,128)} %get-tuple-element.400, f32[512,8]{0,1:T(8,128)S(1)} %select_maximum_fusion.2, pred[512,512]{0,1:T(8,128)(4,1)S(1)} %fusion.43), kind=kLoop, calls=%fused_computation.8.clone.1 | loop fusion | flops 8384512 | bytes 8683520 | tf_op jit(solution)/shard_map/while/body/eval_jaxpr/while/body/eval_jaxpr/reduce_sum | solution.py:76
  216.8 7.7 %bitcast_add_fusion.2 = f32[512,8,128]{0,2,1:T(8,128)} fusion(f32[512,8,128]{0,2,1:T(8,128)} %get-tuple-element.419, bf16[512,8,128]{0,2,1:T(8,128)(2,1)} %bitcast.78, f32[8,512,512]{2,1,0:T(8,128)} %get-tuple-element.400, f32[512,8]{0,1:T(8,128)S(1)} %select_maximum_fusion.2, pred[512,512]{0,1:T(8,128)(4,1)S(1)} %fusion.43, ...), kind=kOutput, calls=%fused_computation.14.clone.1 | convolution fusion | flops 546832384 | bytes 13926401 | tf_op jit(solution)/shard_map/while/body/eval_jaxpr/while/body/eval_jaxpr/qhk,khd->qhd/dot_general | solution.py:77
  231.9 4.2 %all-to-all-start.5 = ((bf16[4,128,1024]{2,1,0:T(8,128)(2,1)}), bf16[4,128,1024]{2,1,0:T(8,128)(2,1)}, u32[]{:S(2)}, u32[]{:S(2)}) async-start(bf16[4,128,1024]{2,1,0:T(8,128)(2,1)} %copy.59), calls=%async_computation.5 | async-start | bytes 2097152 | tf_op jit(solution)/shard_map/all_to_all | solution.py:95
  236.2 25.2 %all-to-all-done.5 = bf16[4,128,1024]{2,1,0:T(8,128)(2,1)} async-done(((bf16[4,128,1024]{2,1,0:T(8,128)(2,1)}), bf16[4,128,1024]{2,1,0:T(8,128)(2,1)}, u32[]{:S(2)}, u32[]{:S(2)}) %all-to-all-start.5) | async-done | bytes 1048608 | tf_op jit(solution)/shard_map/all_to_all | solution.py:95
  266.7 37.1 %all-gather.2.cloned.1.call-done = bf16[128,4096]{1,0:T(8,128)(2,1)} async-done(((bf16[8,4096]{1,0:T(8,128)(2,1)}), bf16[128,4096]{1,0:T(8,128)(2,1)}) %all-gather.2.cloned.1.call-update) | async-done | bytes 1048592 | tf_op jit(solution)/shard_map/all_gather | solution.py:102
  306.6 20.2 %reduce-scatter.2.cloned.1.call-done = bf16[32,1536]{1,0:T(8,128)(2,1)} async-done(((bf16[128,1536]{1,0:T(8,128)(2,1)}), bf16[32,1536]{1,0:T(8,128)(2,1)}) %reduce-scatter.2.cloned.1.call-update) | async-done | bytes 98320 | tf_op jit(solution)/shard_map/reduce_scatter | solution.py:107
  (62 shorter events, 53.5 us)
Async XLA Ops:
  7.2 298.0 %copy-start = (bf16[1024,1536]{1,0:T(8,128)(2,1)S(1)}, bf16[1024,1536]{1,0:T(8,128)(2,1)}, u32[]{:S(2)}) copy-start(bf16[1024,1536]{1,0:T(8,128)(2,1)} %param.13) | copy-start | bytes 9437188
  9.7 32.1 %all-to-all-start.4 = ((bf16[128,4,1024]{0,2,1:T(8,128)(2,1)}), bf16[128,4,1024]{0,2,1:T(8,128)(2,1)}, u32[]{:S(2)}, u32[]{:S(2)}) async-start(bf16[128,4,1024]{0,2,1:T(8,128)(2,1)} %bitcast.81), calls=%async_computation.4 | async-start | bytes 2097152 | tf_op jit(solution)/shard_map/all_to_all | solution.py:40
  43.0 33.9 %copy-start.1 = (bf16[128,1024]{1,0:T(8,128)(2,1)S(1)}, bf16[128,1024]{1,0:T(8,128)(2,1)}, u32[]{:S(2)}) copy-start(bf16[128,1024]{1,0:T(8,128)(2,1)} %param.9) | copy-start | bytes 786436
  43.0 29.7 %all-to-all-start.1 = ((bf16[128,4,1024]{0,2,1:T(8,128)(2,1)}), bf16[128,4,1024]{0,2,1:T(8,128)(2,1)}, u32[]{:S(2)}, u32[]{:S(2)}) async-start(bf16[128,4,1024]{0,2,1:T(8,128)(2,1)} %bitcast.82), calls=%async_computation.1 | async-start | bytes 2097152 | tf_op jit(solution)/shard_map/all_to_all | solution.py:39
  72.7 29.5 %all-to-all-start.2 = ((bf16[128,4,1024]{2,0,1:T(8,128)(2,1)}), bf16[128,4,1024]{2,0,1:T(8,128)(2,1)}, u32[]{:S(2)}, u32[]{:S(2)}) async-start(bf16[128,4,1024]{2,0,1:T(8,128)(2,1)} %bitcast.83), calls=%async_computation.2 | async-start | bytes 2097152 | tf_op jit(solution)/shard_map/all_to_all | solution.py:38
  78.0 2.8 collective-permute-start
  103.4 29.5 %all-to-all-start.3 = ((bf16[128,4,1024]{0,2,1:T(8,128)(2,1)}), bf16[128,4,1024]{0,2,1:T(8,128)(2,1)}, u32[]{:S(2)}, u32[]{:S(2)}) async-start(bf16[128,4,1024]{0,2,1:T(8,128)(2,1)} %bitcast.80), calls=%async_computation.3 | async-start | bytes 2097152 | tf_op jit(solution)/shard_map/all_to_all | solution.py:42
  134.2 29.5 %all-to-all-start = ((bf16[128,4,1024]{0,2,1:T(8,128)(2,1)}), bf16[128,4,1024]{0,2,1:T(8,128)(2,1)}, u32[]{:S(2)}, u32[]{:S(2)}) async-start(bf16[128,4,1024]{0,2,1:T(8,128)(2,1)} %bitcast.79), calls=%async_computation | async-start | bytes 2097152 | tf_op jit(solution)/shard_map/all_to_all | solution.py:41
  227.3 8.9 %copy-start.3 = (s32[8]{0:T(128)S(1)}, s32[8]{0:T(128)}, u32[]{:S(2)}) copy-start(s32[8]{0:T(128)} %param.11) | copy-start | bytes 100
  229.5 36.5 %copy-start.2 = (f32[4096]{0:T(1024)S(1)}, f32[4096]{0:T(1024)}, u32[]{:S(2)}) copy-start(f32[4096]{0:T(1024)} %param.12) | copy-start | bytes 49156
  231.9 29.5 %all-to-all-start.5 = ((bf16[4,128,1024]{2,1,0:T(8,128)(2,1)}), bf16[4,128,1024]{2,1,0:T(8,128)(2,1)}, u32[]{:S(2)}, u32[]{:S(2)}) async-start(bf16[4,128,1024]{2,1,0:T(8,128)(2,1)} %copy.59), calls=%async_computation.5 | async-start | bytes 2097152 | tf_op jit(solution)/shard_map/all_to_all | solution.py:95
  236.1 67.8 %all-gather.2.cloned.1.call-start = ((), (), s32[]{:S(2)}) async-start(), calls=%async_computation.7 | async-start | bytes 1114112 | tf_op jit(solution)/shard_map/all_gather | solution.py:102
  266.7 60.0 %reduce-scatter.2.cloned.1.call-start = ((), (), s32[]{:S(2)}) async-start(), calls=%async_computation.8 | async-start | bytes 491520 | tf_op jit(solution)/shard_map/reduce_scatter | solution.py:107
Sparse Core Ops, SparseCore 0:
  266.8 37.0 all-gather.1
  307.0 19.7 reduce-scatter.1
where the time goes:
time: 335 us; the launch traced here: 334 us
  waiting for transfers between devices  191 us (57%)
  local copies, waits for them, and re-layouts  49.8 us (15%)
  starting transfers between devices  29.1 us (9%)
  matrix products  29 us (9%)
  other arithmetic  20.3 us (6%)
  between operations  14.2 us (4%)
    all_gather x1, waiting for transfers between devices, on_device(): memory_full = lax.all_gather(normed, ('seq', 'tp'), axis=0, tiled=True)  37.1 us
    all_to_all x1, waiting for transfers between devices, on_device(): lax.all_to_all(attended, 'seq', split_axis=0, concat_axis=1, tiled=True)  25.2 us
    all_to_all x1, waiting for transfers between devices, on_device(): lax.all_to_all(widen(values), 'seq', split_axis=1, concat_axis=0, tiled=T...  24.7 us
    all_to_all x1, waiting for transfers between devices, on_device(): lax.all_to_all(widen(shifted[1]), 'seq', split_axis=1, concat_axis=0, til...  24.1 us
    all_to_all x1, waiting for transfers between devices, on_device(): lax.all_to_all(widen(keys), 'seq', split_axis=1, concat_axis=0, tiled=True)  23 us
    reduce_scatter x1, waiting for transfers between devices, on_device(): lax.psum_scatter(jnp.dot(memory_mine, summary_weight, preferred_element_t...  20.2 us
    all_to_all x1, waiting for transfers between devices, on_device(): lax.all_to_all(queries, 'seq', split_axis=1, concat_axis=0, tiled=True)  19.5 us
    all_to_all x1, waiting for transfers between devices, on_device(): lax.all_to_all(widen(shifted[0]), 'seq', split_axis=1, concat_axis=0, til...  15.8 us
  transfers between devices with their start and end apart: 9, of which 9 were waited for; matrix products, arithmetic and copies ran while one was open for 5% of the time, Pallas kernels for 0%

commit v1 on v0

v1 whole, which is shorter than its diff:
```python
import functools
import math

import jax
import jax.numpy as jnp
from jax import lax
from jax.experimental import pallas as pl
from jax.experimental.pallas import tpu as pltpu
from jax.sharding import PartitionSpec as P

D = 4096
HEADS = 32
KV_HEADS = 8
HEAD_DIM = 128
WINDOW = 512
SHARE = HEADS // KV_HEADS
MESH = pl.DeviceIdType.MESH
AHEAD = 3


def kernel(
    n_tp, n_seq, prior,
    q_hbm, k_ref, v_ref, pos_ref, gain_ref, w_hbm,
    enc_ref, sum_ref,
    q_buf, w_buf, kv, bias, picked, mine, mem, part, red,
    local_sem, kv_send, kv_recv, mem_send, mem_recv, red_send, red_recv,
):
    tp = lax.axis_index("tp")
    seq = lax.axis_index("seq")
    me = tp * n_seq + seq
    n = n_tp * n_seq
    rows = k_ref.shape[0]
    span = (prior + 1) * rows
    picks = pos_ref.shape[0]
    width = D // n_tp
    half = width // 2
    cols = sum_ref.shape[1]
    tile = 512 if cols % 512 == 0 else cols

    def device(index):
        return {"tp": index // n_seq, "seq": index % n_seq}

    q_copy = pltpu.make_async_copy(q_hbm, q_buf, local_sem.at[0])
    w_copy = pltpu.make_async_copy(w_hbm, w_buf, local_sem.at[1])
    q_copy.start()
    w_copy.start()

    barrier = pltpu.get_barrier_semaphore()

    @pl.loop(1, n)
    def _(step):
        pl.semaphore_signal(
            barrier, inc=1, device_id=device((me + step) % n), device_id_type=MESH
        )

    for g in range(KV_HEADS):
        kv[g, 0, prior * rows :, :] = k_ref[:, g * HEAD_DIM : (g + 1) * HEAD_DIM]
        kv[g, 1, prior * rows :, :] = v_ref[:, g * HEAD_DIM : (g + 1) * HEAD_DIM]
    for k in range(1, prior + 1):

        @pl.when(me < k)
        def _():
            start = (prior - k) * rows
            kv[:, :, start : start + rows, :] = jnp.zeros(
                (KV_HEADS, 2, rows, HEAD_DIM), jnp.bfloat16
            )

    row = lax.broadcasted_iota(jnp.int32, (rows, span), 0)
    col = lax.broadcasted_iota(jnp.int32, (rows, span), 1) - prior * rows
    seen = (col <= row) & (col > row - WINDOW) & (col + me * rows >= 0)
    bias[...] = jnp.where(seen, 0.0, -jnp.inf).astype(jnp.float32)

    pick_row = lax.broadcasted_iota(jnp.int32, (picks, rows), 0)
    pick_col = lax.broadcasted_iota(jnp.int32, (picks, rows), 1)
    wanted = jnp.zeros((picks, rows), jnp.int32)
    for j in range(picks):
        wanted = jnp.where(pick_row == j, pos_ref[j] - me * rows, wanted)
    choose = jnp.where(pick_col == wanted, 1.0, 0.0).astype(jnp.bfloat16)

    def slot(c, k):
        return kv.at[c, :, pl.ds((prior - k) * rows, rows), :]

    def send(c, k, lands, way, target):
        return pltpu.make_async_remote_copy(
            src_ref=slot(c, k),
            dst_ref=slot(c, lands),
            send_sem=kv_send.at[way, k, c],
            recv_sem=kv_recv.at[lands, c],
            device_id=target,
            device_id_type=MESH,
        )

    def up(c, k):
        return send(c, k, k + 1, 0, {"tp": tp, "seq": seq + 1})

    def down(c, k):
        return send(c, k, k - 1, 1, {"tp": tp, "seq": seq - 1})

    def far(c):
        return send(c, 0, prior, 1, {"tp": tp + 1, "seq": seq + prior - n_seq})

    has_up = seq + 1 < n_seq
    has_far = (seq + prior >= n_seq) & (tp + 1 < n_tp)

    def own(c):
        @pl.when(has_up)
        def _():
            up(c, 0).start()

        @pl.when(has_far)
        def _():
            far(c).start()

    def from_below(c, k):
        @pl.when(seq >= k)
        def _():
            up(c, k - 1).wait_recv()

            if k < prior:

                @pl.when(has_up)
                def _():
                    up(c, k).start()

    def from_before(c, k):
        @pl.when((seq < k) & (tp > 0))
        def _():
            send(c, 0, k, 1, {"tp": tp, "seq": seq}).wait_recv()

            if k >= 2:

                @pl.when(seq >= 1)
                def _():
                    down(c, k).start()

    fold = math.log2(math.e) / HEAD_DIM**0.5

    def attend(g):
        first = pl.multiple_of(g * SHARE * HEAD_DIM, SHARE * HEAD_DIM)
        q_all = q_buf[:, pl.ds(first, SHARE * HEAD_DIM)]
        q_rows = jnp.concatenate(
            [q_all[:, h * HEAD_DIM : (h + 1) * HEAD_DIM] for h in range(SHARE)], axis=0
        )
        scores = lax.dot_general(
            q_rows, kv[g, 0], (((1,), (1,)), ((), ())), preferred_element_type=jnp.float32
        )
        values = kv[g, 1]
        outs = []
        for h in range(SHARE):
            masked = scores[h * rows : (h + 1) * rows] + bias[...]
            peak = jnp.max(masked, axis=1, keepdims=True)
            weights = jnp.exp2((masked - peak) * fold)
            total = jnp.sum(weights, axis=1, keepdims=True)
            mixed = jnp.dot(
                weights.astype(jnp.bfloat16), values, preferred_element_type=jnp.float32
            )
            outs.append((mixed / total).astype(jnp.bfloat16))
        encoded = jnp.concatenate(outs, axis=1)
        enc_ref[:, pl.ds(first, SHARE * HEAD_DIM)] = encoded
        picked[:, pl.ds(first, SHARE * HEAD_DIM)] = jnp.dot(
            choose, encoded, preferred_element_type=jnp.float32
        )

    pl.semaphore_wait(barrier, n - 1)
    for c in range(AHEAD):
        own(c)
    q_copy.wait()

    @pl.loop(0, KV_HEADS + prior - 1)
    def _(t):
        @pl.when(t + AHEAD < KV_HEADS)
        def _():
            own(t + AHEAD)

        for depth in range(1, prior + 1):
            c = t - (depth - 1)

            @pl.when((c >= 0) & (c < KV_HEADS))
            def _():
                from_below(c, depth)
                from_before(c, prior + 1 - depth)

        @pl.when(t >= prior - 1)
        def _():
            attend(t - (prior - 1))

    x = picked[...]
    meansq = jnp.mean(x * x, axis=1, keepdims=True)
    normed = x * lax.rsqrt(meansq + 1e-05) * gain_ref[...]
    for t in range(n_tp):
        left = normed[:, t * width : t * width + half]
        right = normed[:, t * width + half : (t + 1) * width]
        mine[t] = jnp.concatenate((left, right), axis=0).astype(jnp.bfloat16)

    def share(step):
        other = (me + step) % n
        return pltpu.make_async_remote_copy(
            src_ref=mine.at[other // n_seq],
            dst_ref=mem.at[me],
            send_sem=mem_send.at[step],
            recv_sem=mem_recv.at[me],
            device_id=device(other),
            device_id_type=MESH,
        )

    @pl.loop(1, n)
    def _(step):
        share(step).start()

    mem[me] = mine[tp]
    w_copy.wait()

    @pl.loop(1, n)
    def _(step):
        source = (me + step) % n
        pltpu.make_async_remote_copy(
            src_ref=mine.at[0],
            dst_ref=mem.at[source],
            send_sem=mem_send.at[step],
            recv_sem=mem_recv.at[source],
            device_id=device(source),
            device_id_type=MESH,
        ).wait_recv()

    gathered = mem[...].astype(jnp.float32)
    left = gathered[:, :picks].reshape(n * picks, half)
    right = gathered[:, picks:].reshape(n * picks, half)
    memory = jnp.concatenate((left, right), axis=1).astype(jnp.bfloat16)

    def reduce(step, j):
        other = (tp + step) % n_tp
        return pltpu.make_async_remote_copy(
            src_ref=part.at[other, :, pl.ds(j * tile, tile)],
            dst_ref=red.at[tp, :, pl.ds(j * tile, tile)],
            send_sem=red_send.at[step, j],
            recv_sem=red_recv.at[tp, j],
            device_id={"tp": other, "seq": seq},
            device_id_type=MESH,
        )

    for j in range(cols // tile):
        sums = jnp.dot(
            memory, w_buf[:, j * tile : (j + 1) * tile], preferred_element_type=jnp.float32
        )
        part[:, :, j * tile : (j + 1) * tile] = sums.reshape(n_tp, n_seq * picks, tile).astype(
            jnp.bfloat16
        )
        for step in range(1, n_tp):
            reduce(step, j).start()

    for j in range(cols // tile):
        where = slice(j * tile, (j + 1) * tile)
        total = part[tp, :, where].astype(jnp.float32)
        for step in range(1, n_tp):
            source = (tp + step) % n_tp
            pltpu.make_async_remote_copy(
                src_ref=part.at[0, :, pl.ds(j * tile, tile)],
                dst_ref=red.at[source, :, pl.ds(j * tile, tile)],
                send_sem=red_send.at[step, j],
                recv_sem=red_recv.at[source, j],
                device_id={"tp": source, "seq": seq},
                device_id_type=MESH,
            ).wait_recv()
            total = total + red[source, :, where].astype(jnp.float32)
        sum_ref[:, where] = total.astype(jnp.bfloat16)

    for j in range(cols // tile):
        for step in range(1, n_tp):
            reduce(step, j).wait_send()

    @pl.loop(1, n)
    def _(step):
        share(step).wait_send()

    @pl.loop(0, KV_HEADS)
    def _(c):
        @pl.when(has_up)
        def _():
            up(c, 0).wait_send()

        @pl.when(has_far)
        def _():
            far(c).wait_send()

        for k in range(1, prior):

            @pl.when((seq >= k) & has_up)
            def _():
                up(c, k).wait_send()

        for k in range(2, prior + 1):

            @pl.when((seq < k) & (tp > 0) & (seq >= 1))
            def _():
                down(c, k).wait_send()


def on_device(n_tp, n_seq, queries, keys, values, mem_pos, norm_gain, summary_weight):
    rows = queries.shape[0]
    picks = mem_pos.shape[0]
    prior = -(-(WINDOW - 1) // rows)
    n = n_tp * n_seq
    width = summary_weight.shape[0]
    cols = summary_weight.shape[1]
    tiles = cols // 512 if cols % 512 == 0 else 1
    vmem = pl.BlockSpec(memory_space=pltpu.VMEM)
    anywhere = pl.BlockSpec(memory_space=pl.ANY)
    bf16 = jnp.bfloat16
    dma = pltpu.SemaphoreType.DMA
    span = (prior + 1) * rows
    return pl.pallas_call(
        functools.partial(kernel, n_tp, n_seq, prior),
        out_shape=(
            jax.ShapeDtypeStruct((rows, D), bf16),
            jax.ShapeDtypeStruct((n_seq * picks, cols), bf16),
        ),
        in_specs=[
            anywhere, vmem, vmem, pl.BlockSpec(memory_space=pltpu.SMEM), vmem, anywhere,
        ],
        out_specs=(vmem, vmem),
        scratch_shapes=[
            pltpu.VMEM((rows, D), bf16),
            pltpu.VMEM((width, cols), bf16),
            pltpu.VMEM((KV_HEADS, 2, span, HEAD_DIM), bf16),
            pltpu.VMEM((rows, span), jnp.float32),
            pltpu.VMEM((picks, D), jnp.float32),
            pltpu.VMEM((n_tp, 2 * picks, width // 2), bf16),
            pltpu.VMEM((n, 2 * picks, width // 2), bf16),
            pltpu.VMEM((n_tp, n_seq * picks, cols), bf16),
            pltpu.VMEM((n_tp, n_seq * picks, cols), bf16),
            dma((2,)),
            dma((2, prior + 1, KV_HEADS)),
            dma((prior + 1, KV_HEADS)),
            dma((n,)),
            dma((n,)),
            dma((n_tp, tiles)),
            dma((n_tp, tiles)),
        ],
        compiler_params=pltpu.CompilerParams(
            collective_id=0, has_side_effects=True, vmem_limit_bytes=60 * 1024 * 1024
        ),
        cost_estimate=pl.CostEstimate(
            flops=4 * HEADS * rows * span * HEAD_DIM + 2 * n * picks * width * cols,
            bytes_accessed=2 * (2 * rows * D + 4 * rows * KV_HEADS * HEAD_DIM + width * cols),
            transcendentals=HEADS * rows * span,
        ),
    )(queries, keys, values, mem_pos, norm_gain.reshape(1, D), summary_weight)


def solution(mesh):
    placed = (
        P(("file", "tp", "seq"), None),
        P(("file", "tp", "seq"), None),
        P(("file", "tp", "seq"), None),
        P(("file", "tp", "seq")),
        P(),
        P("tp", "seq"),
    )
    return jax.shard_map(
        functools.partial(on_device, mesh.shape["tp"], mesh.shape["seq"]),
        mesh=mesh,
        in_specs=placed,
        out_specs=(P(("file", "tp", "seq"), None), P(("file", "tp"), "seq")),
        check_vma=False,
    )
```

time: 335 us -> 67.2 us (0.20)
  waiting for transfers between devices: 191 us -> 0 us
  Pallas kernels: 0 us -> 61.8 us
  local copies, waits for them, and re-layouts: 49.8 us -> 3.83 us
  starting transfers between devices: 29.1 us -> 0 us
  matrix products: 29 us -> 0 us
  other arithmetic: 20.3 us -> 0 us
  between operations: 14.2 us -> 0.64 us
    all_to_all x6 -> x0, waiting for transfers between devices: 132 us -> none  [the longest x1 25.2 us: on_device(): lax.all_to_all(attended, 'seq', split_axis=0, concat_axis=1, tiled=True)]
    pallas_call x0 -> x1, Pallas kernels: none -> 61.8 us  [on_device(): pl.pallas_call(functools.partial(kernel, n_tp, n_seq, prior), out_shape=(...]
    all_gather x1 -> x0, waiting for transfers between devices: 37.1 us -> none  [on_device(): memory_full = lax.all_gather(normed, ('seq', 'tp'), axis=0, tiled=True)]
    dot_general x5 -> x0, matrix products: 29 us -> none  [the longest x2 14.8 us: step(): jnp.einsum('qhk,khd->qhd', weights.astype(jnp.bfloat16), value_block, pre...]
    all_to_all x6 -> x0, starting transfers between devices: 27.7 us -> none  [the longest x1 6.32 us: on_device(): lax.all_to_all(widen(values), 'seq', split_axis=1, concat_axis=0, tiled=T...]
    reduce_scatter x1 -> x0, waiting for transfers between devices: 20.2 us -> none  [on_device(): lax.psum_scatter(jnp.dot(memory_mine, summary_weight, preferred_element_t...]
    dynamic_slice x6 -> x0, local copies, waits for them, and re-layouts: 15.3 us -> none  [the longest x4 10.7 us: step(): lax.dynamic_slice_in_dim(values_all, k_first, block, 0)]
    all_to_all x6 -> x0, local copies, waits for them, and re-layouts: 13.6 us -> none  [the longest x1 2.29 us: on_device(): lax.all_to_all(attended, 'seq', split_axis=0, concat_axis=1, tiled=True)]
  transfers between devices with their start and end apart: 9 -> 0, of which waited for: 9 -> 0; matrix products, arithmetic and copies ran while one was open for 5% -> 0% of each run, Pallas kernels for 0% -> 0%
where the time goes in v1:
time: 67.2 us; the launch traced here: 66.3 us
  Pallas kernels  61.8 us (92%)
  local copies, waits for them, and re-layouts  3.83 us (6%)
    pallas_call x1, Pallas kernels, on_device(): pl.pallas_call(functools.partial(kernel, n_tp, n_seq, prior), out_shape=(...  61.8 us
    unnamed x2, local copies, waits for them, and re-layouts  3.83 us

profile of v1, /device:TPU:0, one launch (start us, length us, event | category | flops | bytes accessed | tf_op | source)
XLA Modules:
  0.0 66.3 jit_solution(1953057218138886667)
XLA Ops:
  0.6 61.8 %shard_map.77 = (bf16[128,4096]{1,0:T(8,128)(2,1)}, bf16[32,1536]{1,0:T(8,128)(2,1)}) custom-call(bf16[128,4096]{1,0:T(8,128)(2,1)} %q_hbm.1, bf16[128,1024]{1,0:T(8,128)(2,1)} %k_ref.1, bf16[128,1024]{1,0:T(8,128)(2,1)} %v_ref.1, s32[8]{0:T(128)} %pos_ref.1, f32[1,4096]{1,0:T(1,128)} %bitcast.1, bf16[1024,1536]{1,0:T(8,128)(2,1)} %w_hbm.1), custom_call_target="tpu_custom_call" | custom-call | flops 1744830464 | bytes 6291456 | tf_op jit(solution)/shard_map/pallas_call | solution.py:311
  62.4 2.3 %copy.10 = bf16[128,4096]{1,0:T(8,128)(2,1)} copy(bf16[128,4096]{1,0:T(8,128)(2,1)} %get-tuple-element.4) | data formatting | bytes 2097152
  64.7 1.5 %copy.11 = bf16[32,1536]{1,0:T(8,128)(2,1)} copy(bf16[32,1536]{1,0:T(8,128)(2,1)} %get-tuple-element.5) | data formatting | bytes 196608

commit v2 on v1

--- a/solution.py
+++ b/solution.py
@@ -16,14 +16,27 @@
 SHARE = HEADS // KV_HEADS
 MESH = pl.DeviceIdType.MESH
 AHEAD = 3
+PIECES = 4
+
+
+def hand_over(enc_from, sum_from, enc_to, sum_to, sems):
+    rows = enc_from.shape[0] // PIECES
+    copies = [pltpu.make_async_copy(sum_from, sum_to, sems.at[PIECES])]
+    for i in range(PIECES):
+        piece = pl.ds(i * rows, rows)
+        copies.append(pltpu.make_async_copy(enc_from.at[piece], enc_to.at[piece], sems.at[i]))
+    for copy in copies:
+        copy.start()
+    for copy in copies:
+        copy.wait()
 
 
 def kernel(
     n_tp, n_seq, prior,
     q_hbm, k_ref, v_ref, pos_ref, gain_ref, w_hbm,
     enc_ref, sum_ref,
-    q_buf, w_buf, kv, bias, picked, mine, mem, part, red,
-    local_sem, kv_send, kv_recv, mem_send, mem_recv, red_send, red_recv,
+    q_buf, w_buf, kv, bias, squares, mine, mem, sums, part, red, scales,
+    local_sem, kv_send, kv_recv, mem_send, mem_recv, red_send, red_recv, scale_send, scale_recv,
 ):
     tp = lax.axis_index("tp")
     seq = lax.axis_index("seq")
@@ -32,10 +45,13 @@
     rows = k_ref.shape[0]
     span = (prior + 1) * rows
     picks = pos_ref.shape[0]
-    width = D // n_tp
-    half = width // 2
+    per = KV_HEADS // n_tp
+    columns = SHARE * HEAD_DIM
+    half = columns // 2
     cols = sum_ref.shape[1]
     tile = 512 if cols % 512 == 0 else cols
+    squares[...] = jnp.zeros_like(squares)
+    sums[...] = jnp.zeros_like(sums)
 
     def device(index):
         return {"tp": index // n_seq, "seq": index % n_seq}
@@ -157,16 +173,84 @@
             outs.append((mixed / total).astype(jnp.bfloat16))
         encoded = jnp.concatenate(outs, axis=1)
         enc_ref[:, pl.ds(first, SHARE * HEAD_DIM)] = encoded
-        picked[:, pl.ds(first, SHARE * HEAD_DIM)] = jnp.dot(
-            choose, encoded, preferred_element_type=jnp.float32
-        )
+        picked = jnp.dot(choose, encoded, preferred_element_type=jnp.float32)
+        squared = picked * picked
+        for h in range(SHARE):
+            squares[...] += squared[:, h * HEAD_DIM : (h + 1) * HEAD_DIM]
+        gained = picked * gain_ref[:, pl.ds(first, columns)]
+        mine[g] = jnp.concatenate((gained[:, :half], gained[:, half:]), axis=0).astype(jnp.bfloat16)
+
+    def share(g, s, source):
+        return pltpu.make_async_remote_copy(
+            src_ref=mine.at[g],
+            dst_ref=mem.at[g % per, source],
+            send_sem=mem_send.at[g, s],
+            recv_sem=mem_recv.at[g % per, source],
+            device_id={"tp": g // per, "seq": s},
+            device_id_type=MESH,
+        )
+
+    def each_share(g, act):
+        for step in range(1, n_seq):
+            act(share(g, (seq + step) % n_seq, me))
+
+        @pl.when(g // per != tp)
+        def _():
+            act(share(g, seq, me))
+
+    def scale_to(step):
+        return pltpu.make_async_remote_copy(
+            src_ref=scales.at[seq],
+            dst_ref=scales.at[seq],
+            send_sem=scale_send.at[step],
+            recv_sem=scale_recv.at[seq],
+            device_id={"tp": tp, "seq": (seq + step) % n_seq},
+            device_id_type=MESH,
+        )
+
+    def reduce(step):
+        other = (tp + step) % n_tp
+        return pltpu.make_async_remote_copy(
+            src_ref=part.at[other],
+            dst_ref=red.at[tp],
+            send_sem=red_send.at[step],
+            recv_sem=red_recv.at[tp],
+            device_id={"tp": other, "seq": seq},
+            device_id_type=MESH,
+        )
+
+    def project(g):
+        place = g % per
+
+        @pl.loop(1, n)
+        def _(step):
+            source = (me + step) % n
+            share(per * tp + place, seq, source).wait_recv()
+
+        gathered = mem[place].astype(jnp.float32)
+        left = gathered[:, :picks].reshape(n * picks, half)
+        right = gathered[:, picks:].reshape(n * picks, half)
+        memory = jnp.concatenate((left, right), axis=1).astype(jnp.bfloat16)
+        down_to = pl.multiple_of(place * columns, columns)
+        for j in range(cols // tile):
+            where = slice(j * tile, (j + 1) * tile)
+            sums[:, where] += jnp.dot(
+                memory, w_buf[pl.ds(down_to, columns), where], preferred_element_type=jnp.float32
+            )
+
+        @pl.when(place == per - 1)
+        def _():
+            part[...] = sums[...].reshape(n_tp, n_seq * picks, cols).astype(jnp.bfloat16)
+            for step in range(1, n_tp):
+                reduce(step).start()
 
     pl.semaphore_wait(barrier, n - 1)
     for c in range(AHEAD):
         own(c)
     q_copy.wait()
-
-    @pl.loop(0, KV_HEADS + prior - 1)
+    w_copy.wait()
+
+    @pl.loop(0, KV_HEADS + prior)
     def _(t):
         @pl.when(t + AHEAD < KV_HEADS)
         def _():
@@ -180,97 +264,61 @@
                 from_below(c, depth)
                 from_before(c, prior + 1 - depth)
 
-        @pl.when(t >= prior - 1)
-        def _():
-            attend(t - (prior - 1))
-
-    x = picked[...]
-    meansq = jnp.mean(x * x, axis=1, keepdims=True)
-    normed = x * lax.rsqrt(meansq + 1e-05) * gain_ref[...]
-    for t in range(n_tp):
-        left = normed[:, t * width : t * width + half]
-        right = normed[:, t * width + half : (t + 1) * width]
-        mine[t] = jnp.concatenate((left, right), axis=0).astype(jnp.bfloat16)
-
-    def share(step):
-        other = (me + step) % n
-        return pltpu.make_async_remote_copy(
-            src_ref=mine.at[other // n_seq],
-            dst_ref=mem.at[me],
-            send_sem=mem_send.at[step],
-            recv_sem=mem_recv.at[me],
-            device_id=device(other),
-            device_id_type=MESH,
-        )
-
-    @pl.loop(1, n)
-    def _(step):
-        share(step).start()
-
-    mem[me] = mine[tp]
-    w_copy.wait()
-
-    @pl.loop(1, n)
-    def _(step):
-        source = (me + step) % n
+        g = t - (prior - 1)
+
+        @pl.when((g >= 0) & (g < KV_HEADS))
+        def _():
+            attend(g)
+            each_share(g, lambda copy: copy.start())
+
+            @pl.when(g // per == tp)
+            def _():
+                mem[g % per, me] = mine[g]
+
+        @pl.when(g == KV_HEADS - 1)
+        def _():
+            meansq = jnp.sum(squares[...], axis=1, keepdims=True) / D
+            scales[seq] = jnp.broadcast_to(lax.rsqrt(meansq + 1e-05), scales.shape[1:])
+            for step in range(1, n_seq):
+                scale_to(step).start()
+
+        @pl.when((g >= 1) & ((g - 1) // per == tp))
+        def _():
+            project(g - 1)
+
+    total = part[tp].astype(jnp.float32)
+    for step in range(1, n_tp):
+        source = (tp + step) % n_tp
         pltpu.make_async_remote_copy(
-            src_ref=mine.at[0],
-            dst_ref=mem.at[source],
-            send_sem=mem_send.at[step],
-            recv_sem=mem_recv.at[source],
-            device_id=device(source),
+            src_ref=part.at[0],
+            dst_ref=red.at[source],
+            send_sem=red_send.at[step],
+            recv_sem=red_recv.at[source],
+            device_id={"tp": source, "seq": seq},
             device_id_type=MESH,
         ).wait_recv()
-
-    gathered = mem[...].astype(jnp.float32)
-    left = gathered[:, :picks].reshape(n * picks, half)
-    right = gathered[:, picks:].reshape(n * picks, half)
-    memory = jnp.concatenate((left, right), axis=1).astype(jnp.bfloat16)
-
-    def reduce(step, j):
-        other = (tp + step) % n_tp
-        return pltpu.make_async_remote_copy(
-            src_ref=part.at[other, :, pl.ds(j * tile, tile)],
-            dst_ref=red.at[tp, :, pl.ds(j * tile, tile)],
-            send_sem=red_send.at[step, j],
-            recv_sem=red_recv.at[tp, j],
-            device_id={"tp": other, "seq": seq},
-            device_id_type=MESH,
-        )
-
-    for j in range(cols // tile):
-        sums = jnp.dot(
-            memory, w_buf[:, j * tile : (j + 1) * tile], preferred_element_type=jnp.float32
-        )
-        part[:, :, j * tile : (j + 1) * tile] = sums.reshape(n_tp, n_seq * picks, tile).astype(
-            jnp.bfloat16
-        )
-        for step in range(1, n_tp):
-            reduce(step, j).start()
-
-    for j in range(cols // tile):
-        where = slice(j * tile, (j + 1) * tile)
-        total = part[tp, :, where].astype(jnp.float32)
-        for step in range(1, n_tp):
-            source = (tp + step) % n_tp
-            pltpu.make_async_remote_copy(
-                src_ref=part.at[0, :, pl.ds(j * tile, tile)],
-                dst_ref=red.at[source, :, pl.ds(j * tile, tile)],
-                send_sem=red_send.at[step, j],
-                recv_sem=red_recv.at[source, j],
-                device_id={"tp": source, "seq": seq},
-                device_id_type=MESH,
-            ).wait_recv()
-            total = total + red[source, :, where].astype(jnp.float32)
-        sum_ref[:, where] = total.astype(jnp.bfloat16)
-
-    for j in range(cols // tile):
-        for step in range(1, n_tp):
-            reduce(step, j).wait_send()
-
-    @pl.loop(1, n)
-    def _(step):
-        share(step).wait_send()
+        total = total + red[source].astype(jnp.float32)
+    for step in range(1, n_seq):
+        source = (seq + step) % n_seq
+        pltpu.make_async_remote_copy(
+            src_ref=scales.at[source],
+            dst_ref=scales.at[source],
+            send_sem=scale_send.at[step],
+            recv_sem=scale_recv.at[source],
+            device_id={"tp": tp, "seq": source},
+            device_id_type=MESH,
+        ).wait_recv()
+    factor = scales[...].reshape(n_seq * picks, HEAD_DIM)[:, :1]
+    sum_ref[...] = (total * factor).astype(jnp.bfloat16)
+
+    for step in range(1, n_tp):
+        reduce(step).wait_send()
+    for step in range(1, n_seq):
+        scale_to(step).wait_send()
+
+    @pl.loop(0, KV_HEADS)
+    def _(g):
+        each_share(g, lambda copy: copy.wait_send())
 
     @pl.loop(0, KV_HEADS)
     def _(c):
@@ -302,13 +350,14 @@
     n = n_tp * n_seq
     width = summary_weight.shape[0]
     cols = summary_weight.shape[1]
-    tiles = cols // 512 if cols % 512 == 0 else 1
+    per = KV_HEADS // n_tp
+    half = width // per // 2
     vmem = pl.BlockSpec(memory_space=pltpu.VMEM)
     anywhere = pl.BlockSpec(memory_space=pl.ANY)
     bf16 = jnp.bfloat16
     dma = pltpu.SemaphoreType.DMA
     span = (prior + 1) * rows
-    return pl.pallas_call(
+    results = pl.pallas_call(
         functools.partial(kernel, n_tp, n_seq, prior),
         out_shape=(
             jax.ShapeDtypeStruct((rows, D), bf16),
@@ -323,18 +372,22 @@
             pltpu.VMEM((width, cols), bf16),
             pltpu.VMEM((KV_HEADS, 2, span, HEAD_DIM), bf16),
             pltpu.VMEM((rows, span), jnp.float32),
-            pltpu.VMEM((picks, D), jnp.float32),
-            pltpu.VMEM((n_tp, 2 * picks, width // 2), bf16),
-            pltpu.VMEM((n, 2 * picks, width // 2), bf16),
+            pltpu.VMEM((picks, HEAD_DIM), jnp.float32),
+            pltpu.VMEM((KV_HEADS, 2 * picks, half), bf16),
+            pltpu.VMEM((per, n, 2 * picks, half), bf16),
+            pltpu.VMEM((n * picks, cols), jnp.float32),
             pltpu.VMEM((n_tp, n_seq * picks, cols), bf16),
             pltpu.VMEM((n_tp, n_seq * picks, cols), bf16),
+            pltpu.VMEM((n_seq, picks, HEAD_DIM), jnp.float32),
             dma((2,)),
             dma((2, prior + 1, KV_HEADS)),
             dma((prior + 1, KV_HEADS)),
-            dma((n,)),
-            dma((n,)),
-            dma((n_tp, tiles)),
-            dma((n_tp, tiles)),
+            dma((KV_HEADS, n_seq)),
+            dma((per, n)),
+            dma((n_tp,)),
+            dma((n_tp,)),
+            dma((n_seq,)),
+            dma((n_seq,)),
         ],
         compiler_params=pltpu.CompilerParams(
             collective_id=0, has_side_effects=True, vmem_limit_bytes=60 * 1024 * 1024
@@ -345,6 +398,14 @@
             transcendentals=HEADS * rows * span,
         ),
     )(queries, keys, values, mem_pos, norm_gain.reshape(1, D), summary_weight)
+    return pl.pallas_call(
+        hand_over,
+        out_shape=tuple(jax.ShapeDtypeStruct(r.shape, r.dtype) for r in results),
+        in_specs=[anywhere, anywhere],
+        out_specs=(anywhere, anywhere),
+        scratch_shapes=[dma((PIECES + 1,))],
+        compiler_params=pltpu.CompilerParams(vmem_limit_bytes=60 * 1024 * 1024),
+    )(*results)
 
 
 def solution(mesh):

time: 67.2 us -> 99.8 us (1.49)
  Pallas kernels: 61.8 us -> 98.5 us
  local copies, waits for them, and re-layouts: 3.83 us -> 0 us
    pallas_call x0 -> x1, Pallas kernels: none -> 35.9 us  [on_device(): pl.pallas_call(hand_over, out_shape=tuple((jax.ShapeDtypeStruct(r.shape,...]
    unnamed x2 -> x0, local copies, waits for them, and re-layouts: 3.83 us -> none
where the time goes in v2:
time: 99.8 us; the launch traced here: 99.1 us
  Pallas kernels  98.5 us (99%)
    pallas_call x1, Pallas kernels, on_device(): pl.pallas_call(functools.partial(kernel, n_tp, n_seq, prior), out_shape=(...  62.6 us
    pallas_call x1, Pallas kernels, on_device(): pl.pallas_call(hand_over, out_shape=tuple((jax.ShapeDtypeStruct(r.shape,...  35.9 us

profile of v2, /device:TPU:0, one launch (start us, length us, event | category | flops | bytes accessed | tf_op | source)
XLA Modules:
  0.0 99.1 jit_solution(4001780760808205875)
XLA Ops:
  0.6 62.6 %shard_map.77 = (bf16[128,4096]{1,0:T(8,128)(2,1)}, bf16[32,1536]{1,0:T(8,128)(2,1)}) custom-call(bf16[128,4096]{1,0:T(8,128)(2,1)} %q_hbm.1, bf16[128,1024]{1,0:T(8,128)(2,1)} %k_ref.1, bf16[128,1024]{1,0:T(8,128)(2,1)} %v_ref.1, s32[8]{0:T(128)} %pos_ref.1, f32[1,4096]{1,0:T(1,128)} %bitcast.1, bf16[1024,1536]{1,0:T(8,128)(2,1)} %w_hbm.1), custom_call_target="tpu_custom_call" | custom-call | flops 1744830464 | bytes 6291456 | tf_op jit(solution)/shard_map/pallas_call | solution.py:360
  63.2 35.9 %shard_map.78 = (bf16[128,4096]{1,0:T(8,128)(2,1)}, bf16[32,1536]{1,0:T(8,128)(2,1)}) custom-call(bf16[128,4096]{1,0:T(8,128)(2,1)} %get-tuple-element.4.enc_from, bf16[32,1536]{1,0:T(8,128)(2,1)} %get-tuple-element.5.sum_from), custom_call_target="tpu_custom_call" | custom-call | tf_op jit(solution)/shard_map/pallas_call | solution.py:401

commit v3 on v2

--- a/solution.py
+++ b/solution.py
@@ -19,15 +19,20 @@
 PIECES = 4
 
 
-def hand_over(enc_from, sum_from, enc_to, sum_to, sems):
+def hand_over(enc_from, sum_from, enc_to, sum_to, enc_buf, sum_buf, sems):
     rows = enc_from.shape[0] // PIECES
-    copies = [pltpu.make_async_copy(sum_from, sum_to, sems.at[PIECES])]
+    parts = [(sum_from, sum_buf, sum_to)]
     for i in range(PIECES):
         piece = pl.ds(i * rows, rows)
-        copies.append(pltpu.make_async_copy(enc_from.at[piece], enc_to.at[piece], sems.at[i]))
-    for copy in copies:
+        parts.append((enc_from.at[piece], enc_buf.at[piece], enc_to.at[piece]))
+    into = [pltpu.make_async_copy(a, b, sems.at[0, i]) for i, (a, b, c) in enumerate(parts)]
+    out = [pltpu.make_async_copy(b, c, sems.at[1, i]) for i, (a, b, c) in enumerate(parts)]
+    for copy in into:
         copy.start()
-    for copy in copies:
+    for first, second in zip(into, out):
+        first.wait()
+        second.start()
+    for copy in out:
         copy.wait()
 
 
@@ -403,7 +408,10 @@
         out_shape=tuple(jax.ShapeDtypeStruct(r.shape, r.dtype) for r in results),
         in_specs=[anywhere, anywhere],
         out_specs=(anywhere, anywhere),
-        scratch_shapes=[dma((PIECES + 1,))],
+        scratch_shapes=[
+            *(pltpu.VMEM(r.shape, r.dtype) for r in results),
+            dma((2, PIECES + 1)),
+        ],
         compiler_params=pltpu.CompilerParams(vmem_limit_bytes=60 * 1024 * 1024),
     )(*results)
 

time: 99.8 us -> 65.9 us (0.66)
  Pallas kernels: 98.5 us -> 64.6 us
    pallas_call x1, Pallas kernels: 35.9 us -> 2.05 us  [on_device(): pl.pallas_call(hand_over, out_shape=tuple((jax.ShapeDtypeStruct(r.shape,...]
where the time goes in v3:
time: 65.9 us; the launch traced here: 65.3 us
  Pallas kernels  64.6 us (98%)
    pallas_call x1, Pallas kernels, on_device(): pl.pallas_call(functools.partial(kernel, n_tp, n_seq, prior), out_shape=(...  62.6 us
    pallas_call x1, Pallas kernels, on_device(): pl.pallas_call(hand_over, out_shape=tuple((jax.ShapeDtypeStruct(r.shape,...  2.05 us

profile of v3, /device:TPU:0, one launch (start us, length us, event | category | flops | bytes accessed | tf_op | source)
XLA Modules:
  0.0 65.3 jit_solution(2862504623887999325)
XLA Ops:
  0.6 62.6 %shard_map.77 = (bf16[128,4096]{1,0:T(8,128)(2,1)}, bf16[32,1536]{1,0:T(8,128)(2,1)}) custom-call(bf16[128,4096]{1,0:T(8,128)(2,1)} %q_hbm.1, bf16[128,1024]{1,0:T(8,128)(2,1)} %k_ref.1, bf16[128,1024]{1,0:T(8,128)(2,1)} %v_ref.1, s32[8]{0:T(128)} %pos_ref.1, f32[1,4096]{1,0:T(1,128)} %bitcast.1, bf16[1024,1536]{1,0:T(8,128)(2,1)} %w_hbm.1), custom_call_target="tpu_custom_call" | custom-call | flops 1744830464 | bytes 6291456 | tf_op jit(solution)/shard_map/pallas_call | solution.py:365
  63.2 2.1 %shard_map.78 = (bf16[128,4096]{1,0:T(8,128)(2,1)}, bf16[32,1536]{1,0:T(8,128)(2,1)}) custom-call(bf16[128,4096]{1,0:T(8,128)(2,1)} %get-tuple-element.4.enc_from, bf16[32,1536]{1,0:T(8,128)(2,1)} %get-tuple-element.5.sum_from), custom_call_target="tpu_custom_call" | custom-call | tf_op jit(solution)/shard_map/pallas_call | solution.py:406

commit v4 on v3

--- a/solution.py
+++ b/solution.py
@@ -40,8 +40,10 @@
     n_tp, n_seq, prior,
     q_hbm, k_ref, v_ref, pos_ref, gain_ref, w_hbm,
     enc_ref, sum_ref,
-    q_buf, w_buf, kv, bias, squares, mine, mem, sums, part, red, scales,
+    q_buf, w_buf, kv, bias, help_bias, squares, mine, mem, sums, part, red, scales,
+    help_q, help_out, returned,
     local_sem, kv_send, kv_recv, mem_send, mem_recv, red_send, red_recv, scale_send, scale_recv,
+    query_send, query_recv, back_send, back_recv,
 ):
     tp = lax.axis_index("tp")
     seq = lax.axis_index("seq")
@@ -61,6 +63,15 @@
     def device(index):
         return {"tp": index // n_seq, "seq": index % n_seq}
 
+    is_top = seq == n_seq - 1
+    is_bottom = (seq == 0) & (tp > 0)
+    asks = is_top | is_bottom
+    helps_top = seq == n_seq - 2
+    helps_bottom = (seq == 1) & (tp > 0)
+    helps = helps_top | helps_bottom
+    inward = 1 - 2 * (seq // (n_seq - 1))
+    outward = 2 * ((seq - 1) // (n_seq - 3)) - 1
+
     q_copy = pltpu.make_async_copy(q_hbm, q_buf, local_sem.at[0])
     w_copy = pltpu.make_async_copy(w_hbm, w_buf, local_sem.at[1])
     q_copy.start()
@@ -75,21 +86,23 @@
         )
 
     for g in range(KV_HEADS):
-        kv[g, 0, prior * rows :, :] = k_ref[:, g * HEAD_DIM : (g + 1) * HEAD_DIM]
-        kv[g, 1, prior * rows :, :] = v_ref[:, g * HEAD_DIM : (g + 1) * HEAD_DIM]
+        kv[g, 0, (prior + 1) * rows : (prior + 2) * rows, :] = k_ref[:, g * HEAD_DIM : (g + 1) * HEAD_DIM]
+        kv[g, 1, (prior + 1) * rows : (prior + 2) * rows, :] = v_ref[:, g * HEAD_DIM : (g + 1) * HEAD_DIM]
     for k in range(1, prior + 1):
 
         @pl.when(me < k)
         def _():
-            start = (prior - k) * rows
+            start = (prior + 1 - k) * rows
             kv[:, :, start : start + rows, :] = jnp.zeros(
                 (KV_HEADS, 2, rows, HEAD_DIM), jnp.bfloat16
             )
 
     row = lax.broadcasted_iota(jnp.int32, (rows, span), 0)
     col = lax.broadcasted_iota(jnp.int32, (rows, span), 1) - prior * rows
-    seen = (col <= row) & (col > row - WINDOW) & (col + me * rows >= 0)
-    bias[...] = jnp.where(seen, 0.0, -jnp.inf).astype(jnp.float32)
+    band = (col <= row) & (col > row - WINDOW)
+    bias[...] = jnp.where(band & (col + me * rows >= 0), 0.0, -jnp.inf).astype(jnp.float32)
+    help_seen = band & (col + (me + outward) * rows >= 0)
+    help_bias[...] = jnp.where(help_seen, 0.0, -jnp.inf).astype(jnp.float32)
 
     pick_row = lax.broadcasted_iota(jnp.int32, (picks, rows), 0)
     pick_col = lax.broadcasted_iota(jnp.int32, (picks, rows), 1)
@@ -99,14 +112,14 @@
     choose = jnp.where(pick_col == wanted, 1.0, 0.0).astype(jnp.bfloat16)
 
     def slot(c, k):
-        return kv.at[c, :, pl.ds((prior - k) * rows, rows), :]
+        return kv.at[c, :, pl.ds((prior + 1 - k) * rows, rows), :]
 
     def send(c, k, lands, way, target):
         return pltpu.make_async_remote_copy(
             src_ref=slot(c, k),
             dst_ref=slot(c, lands),
             send_sem=kv_send.at[way, k, c],
-            recv_sem=kv_recv.at[lands, c],
+            recv_sem=kv_recv.at[lands + 1, c],
             device_id=target,
             device_id_type=MESH,
         )
@@ -120,52 +133,113 @@
     def far(c):
         return send(c, 0, prior, 1, {"tp": tp + 1, "seq": seq + prior - n_seq})
 
-    has_up = seq + 1 < n_seq
+    def extra_down(c):
+        return send(c, 0, -1, 2, {"tp": tp, "seq": seq - 1})
+
+    def extra_up(c):
+        return send(c, prior, prior + 1, 2, {"tp": tp, "seq": seq + 1})
+
+    def ask(c):
+        return pltpu.make_async_remote_copy(
+            src_ref=q_buf.at[:, pl.ds(pl.multiple_of(c * columns, columns), columns)],
+            dst_ref=help_q.at[c // 2],
+            send_sem=query_send.at[c // 2],
+            recv_sem=query_recv.at[c // 2],
+            device_id={"tp": tp, "seq": seq + inward},
+            device_id_type=MESH,
+        )
+
+    def give_back(c):
+        return pltpu.make_async_remote_copy(
+            src_ref=help_out.at[c // 2],
+            dst_ref=returned.at[c // 2],
+            send_sem=back_send.at[c // 2],
+            recv_sem=back_recv.at[c // 2],
+            device_id={"tp": tp, "seq": seq + outward},
+            device_id_type=MESH,
+        )
+
+    def has_up(c):
+        return seq + 1 + c % 2 < n_seq
+
+    def has_down(c):
+        return seq >= 1 + c % 2
+
     has_far = (seq + prior >= n_seq) & (tp + 1 < n_tp)
 
+    def each_own(c, act):
+        @pl.when(has_up(c))
+        def _():
+            act(up(c, 0))
+
+        @pl.when(has_far)
+        def _():
+            act(far(c))
+
+        @pl.when(asks & (c % 2 == 1))
+        def _():
+            act(ask(c))
+
+        @pl.when(is_top & (c % 2 == 1))
+        def _():
+            act(extra_down(c))
+
     def own(c):
-        @pl.when(has_up)
-        def _():
-            up(c, 0).start()
-
-        @pl.when(has_far)
-        def _():
-            far(c).start()
+        each_own(c, lambda copy: copy.start())
 
     def from_below(c, k):
-        @pl.when(seq >= k)
+        @pl.when((seq >= k) & (seq + c % 2 < n_seq))
         def _():
             up(c, k - 1).wait_recv()
 
             if k < prior:
 
-                @pl.when(has_up)
+                @pl.when(has_up(c))
                 def _():
                     up(c, k).start()
 
+        if k == 1:
+
+            @pl.when(helps_top & (c % 2 == 1))
+            def _():
+                extra_down(c).wait_recv()
+
     def from_before(c, k):
-        @pl.when((seq < k) & (tp > 0))
+        arrives = (seq < k) & (tp > 0)
+        if k < prior:
+            arrives = arrives & (seq >= c % 2)
+
+        @pl.when(arrives)
         def _():
             send(c, 0, k, 1, {"tp": tp, "seq": seq}).wait_recv()
 
             if k >= 2:
 
-                @pl.when(seq >= 1)
+                @pl.when(has_down(c))
                 def _():
                     down(c, k).start()
 
+            if k == prior:
+
+                @pl.when(is_bottom & (c % 2 == 1))
+                def _():
+                    extra_up(c).start()
+
+        if k == prior - 1:
+
+            @pl.when(helps_bottom & (c % 2 == 1))
+            def _():
+                extra_up(c).wait_recv()
+
     fold = math.log2(math.e) / HEAD_DIM**0.5
 
-    def attend(g):
-        first = pl.multiple_of(g * SHARE * HEAD_DIM, SHARE * HEAD_DIM)
-        q_all = q_buf[:, pl.ds(first, SHARE * HEAD_DIM)]
+    def attend(q_all, keys, values, bias):
         q_rows = jnp.concatenate(
             [q_all[:, h * HEAD_DIM : (h + 1) * HEAD_DIM] for h in range(SHARE)], axis=0
         )
         scores = lax.dot_general(
-            q_rows, kv[g, 0], (((1,), (1,)), ((), ())), preferred_element_type=jnp.float32
-        )
-        values = kv[g, 1]
+            q_rows, keys, (((1,), (1,)), ((), ())), preferred_element_type=jnp.float32
+        )
         outs = []
         for h in range(SHARE):
             masked = scores[h * rows : (h + 1) * rows] + bias[...]
@@ -176,8 +250,36 @@
                 weights.astype(jnp.bfloat16), values, preferred_element_type=jnp.float32
             )
             outs.append((mixed / total).astype(jnp.bfloat16))
-        encoded = jnp.concatenate(outs, axis=1)
-        enc_ref[:, pl.ds(first, SHARE * HEAD_DIM)] = encoded
+        return jnp.concatenate(outs, axis=1)
+
+    def encode(g):
+        first = pl.multiple_of(g * columns, columns)
+        theirs = asks & (g % 2 == 1)
+
+        @pl.when(helps & (g % 2 == 1))
+        def _():
+            ask(g).wait_recv()
+            reach = pl.ds(pl.multiple_of((1 + outward) * rows, rows), span)
+            help_out[g // 2] = attend(
+                help_q[g // 2], kv[g, 0, reach], kv[g, 1, reach], help_bias
+            )
+            give_back(g).start()
+
+        @pl.when(jnp.logical_not(theirs))
+        def _():
+            enc_ref[:, pl.ds(first, columns)] = attend(
+                q_buf[:, pl.ds(first, columns)],
+                kv[g, 0, rows : rows + span],
+                kv[g, 1, rows : rows + span],
+                bias,
+            )
+
+        @pl.when(theirs)
+        def _():
+            give_back(g).wait_recv()
+            enc_ref[:, pl.ds(first, columns)] = returned[g // 2]
+
+        encoded = enc_ref[:, pl.ds(first, columns)]
         picked = jnp.dot(choose, encoded, preferred_element_type=jnp.float32)
         squared = picked * picked
         for h in range(SHARE):
@@ -250,9 +352,9 @@
                 reduce(step).start()
 
     pl.semaphore_wait(barrier, n - 1)
+    q_copy.wait()
     for c in range(AHEAD):
         own(c)
-    q_copy.wait()
     w_copy.wait()
 
     @pl.loop(0, KV_HEADS + prior)
@@ -273,7 +375,7 @@
 
         @pl.when((g >= 0) & (g < KV_HEADS))
         def _():
-            attend(g)
+            encode(g)
             each_share(g, lambda copy: copy.start())
 
             @pl.when(g // per == tp)
@@ -327,25 +429,27 @@
 
     @pl.loop(0, KV_HEADS)
     def _(c):
-        @pl.when(has_up)
-        def _():
-            up(c, 0).wait_send()
-
-        @pl.when(has_far)
-        def _():
-            far(c).wait_send()
+        each_own(c, lambda copy: copy.wait_send())
 
         for k in range(1, prior):
 
-            @pl.when((seq >= k) & has_up)
+            @pl.when((seq >= k) & has_up(c))
             def _():
                 up(c, k).wait_send()
 
         for k in range(2, prior + 1):
 
-            @pl.when((seq < k) & (tp > 0) & (seq >= 1))
+            @pl.when((seq < k) & (tp > 0) & has_down(c))
             def _():
                 down(c, k).wait_send()
+
+        @pl.when(is_bottom & (c % 2 == 1))
+        def _():
+            extra_up(c).wait_send()
+
+        @pl.when(helps & (c % 2 == 1))
+        def _():
+            give_back(c).wait_send()
 
 
 def on_device(n_tp, n_seq, queries, keys, values, mem_pos, norm_gain, summary_weight):
@@ -375,7 +479,8 @@
         scratch_shapes=[
             pltpu.VMEM((rows, D), bf16),
             pltpu.VMEM((width, cols), bf16),
-            pltpu.VMEM((KV_HEADS, 2, span, HEAD_DIM), bf16),
+            pltpu.VMEM((KV_HEADS, 2, (prior + 3) * rows, HEAD_DIM), bf16),
+            pltpu.VMEM((rows, span), jnp.float32),
             pltpu.VMEM((rows, span), jnp.float32),
             pltpu.VMEM((picks, HEAD_DIM), jnp.float32),
             pltpu.VMEM((KV_HEADS, 2 * picks, half), bf16),
@@ -384,15 +489,22 @@
             pltpu.VMEM((n_tp, n_seq * picks, cols), bf16),
             pltpu.VMEM((n_tp, n_seq * picks, cols), bf16),
             pltpu.VMEM((n_seq, picks, HEAD_DIM), jnp.float32),
+            pltpu.VMEM((KV_HEADS // 2, rows, D // KV_HEADS), bf16),
+            pltpu.VMEM((KV_HEADS // 2, rows, D // KV_HEADS), bf16),
+            pltpu.VMEM((KV_HEADS // 2, rows, D // KV_HEADS), bf16),
             dma((2,)),
-            dma((2, prior + 1, KV_HEADS)),
-            dma((prior + 1, KV_HEADS)),
+            dma((3, prior + 1, KV_HEADS)),
+            dma((prior + 3, KV_HEADS)),
             dma((KV_HEADS, n_seq)),
             dma((per, n)),
             dma((n_tp,)),
             dma((n_tp,)),
             dma((n_seq,)),
             dma((n_seq,)),
+            dma((KV_HEADS // 2,)),
+            dma((KV_HEADS // 2,)),
+            dma((KV_HEADS // 2,)),
+            dma((KV_HEADS // 2,)),
         ],
         compiler_params=pltpu.CompilerParams(
             collective_id=0, has_side_effects=True, vmem_limit_bytes=60 * 1024 * 1024

time: 65.9 us -> 78.8 us (1.20)
  Pallas kernels: 64.6 us -> 77.5 us
    pallas_call x1, Pallas kernels: 62.6 us -> 75.5 us  [on_device(): pl.pallas_call(functools.partial(kernel, n_tp, n_seq, prior), out_shape=(...]
where the time goes in v4:
time: 78.8 us; the launch traced here: 78.2 us
  Pallas kernels  77.5 us (98%)
    pallas_call x1, Pallas kernels, on_device(): pl.pallas_call(functools.partial(kernel, n_tp, n_seq, prior), out_shape=(...  75.5 us
    pallas_call x1, Pallas kernels, on_device(): pl.pallas_call(hand_over, out_shape=tuple((jax.ShapeDtypeStruct(r.shape,...  2.05 us

profile of v4, /device:TPU:0, one launch (start us, length us, event | category | flops | bytes accessed | tf_op | source)
XLA Modules:
  0.0 78.2 jit_solution(12575612868233656013)
XLA Ops:
  0.6 75.5 %shard_map.77 = (bf16[128,4096]{1,0:T(8,128)(2,1)}, bf16[32,1536]{1,0:T(8,128)(2,1)}) custom-call(bf16[128,4096]{1,0:T(8,128)(2,1)} %q_hbm.1, bf16[128,1024]{1,0:T(8,128)(2,1)} %k_ref.1, bf16[128,1024]{1,0:T(8,128)(2,1)} %v_ref.1, s32[8]{0:T(128)} %pos_ref.1, f32[1,4096]{1,0:T(1,128)} %bitcast.1, bf16[1024,1536]{1,0:T(8,128)(2,1)} %w_hbm.1), custom_call_target="tpu_custom_call" | custom-call | flops 1744830464 | bytes 6291456 | tf_op jit(solution)/shard_map/pallas_call | solution.py:469
  76.1 2.1 %shard_map.78 = (bf16[128,4096]{1,0:T(8,128)(2,1)}, bf16[32,1536]{1,0:T(8,128)(2,1)}) custom-call(bf16[128,4096]{1,0:T(8,128)(2,1)} %get-tuple-element.4.enc_from, bf16[32,1536]{1,0:T(8,128)(2,1)} %get-tuple-element.5.sum_from), custom_call_target="tpu_custom_call" | custom-call | tf_op jit(solution)/shard_map/pallas_call | solution.py:518

commit v5 on v3

--- a/solution.py
+++ b/solution.py
@@ -48,6 +48,7 @@
     me = tp * n_seq + seq
     n = n_tp * n_seq
     rows = k_ref.shape[0]
+    assert rows == HEAD_DIM
     span = (prior + 1) * rows
     picks = pos_ref.shape[0]
     per = KV_HEADS // n_tp
@@ -76,7 +77,7 @@
 
     for g in range(KV_HEADS):
         kv[g, 0, prior * rows :, :] = k_ref[:, g * HEAD_DIM : (g + 1) * HEAD_DIM]
-        kv[g, 1, prior * rows :, :] = v_ref[:, g * HEAD_DIM : (g + 1) * HEAD_DIM]
+        kv[g, 1, prior * rows :, :] = v_ref[:, g * HEAD_DIM : (g + 1) * HEAD_DIM].T
     for k in range(1, prior + 1):
 
         @pl.when(me < k)
@@ -86,8 +87,8 @@
                 (KV_HEADS, 2, rows, HEAD_DIM), jnp.bfloat16
             )
 
-    row = lax.broadcasted_iota(jnp.int32, (rows, span), 0)
-    col = lax.broadcasted_iota(jnp.int32, (rows, span), 1) - prior * rows
+    row = lax.broadcasted_iota(jnp.int32, (span, rows), 1)
+    col = lax.broadcasted_iota(jnp.int32, (span, rows), 0) - prior * rows
     seen = (col <= row) & (col > row - WINDOW) & (col + me * rows >= 0)
     bias[...] = jnp.where(seen, 0.0, -jnp.inf).astype(jnp.float32)
 
@@ -156,28 +157,30 @@
 
     fold = math.log2(math.e) / HEAD_DIM**0.5
 
-    def attend(g):
-        first = pl.multiple_of(g * SHARE * HEAD_DIM, SHARE * HEAD_DIM)
-        q_all = q_buf[:, pl.ds(first, SHARE * HEAD_DIM)]
+    def attend(q_all, keys, flipped, bias):
         q_rows = jnp.concatenate(
             [q_all[:, h * HEAD_DIM : (h + 1) * HEAD_DIM] for h in range(SHARE)], axis=0
         )
         scores = lax.dot_general(
-            q_rows, kv[g, 0], (((1,), (1,)), ((), ())), preferred_element_type=jnp.float32
-        )
-        values = kv[g, 1]
-        outs = []
-        for h in range(SHARE):
-            masked = scores[h * rows : (h + 1) * rows] + bias[...]
-            peak = jnp.max(masked, axis=1, keepdims=True)
-            weights = jnp.exp2((masked - peak) * fold)
-            total = jnp.sum(weights, axis=1, keepdims=True)
-            mixed = jnp.dot(
-                weights.astype(jnp.bfloat16), values, preferred_element_type=jnp.float32
-            )
-            outs.append((mixed / total).astype(jnp.bfloat16))
-        encoded = jnp.concatenate(outs, axis=1)
-        enc_ref[:, pl.ds(first, SHARE * HEAD_DIM)] = encoded
+            keys, q_rows, (((1,), (1,)), ((), ())), preferred_element_type=jnp.float32
+        )
+        masked = scores + jnp.concatenate([bias[...]] * SHARE, axis=1)
+        peak = jnp.max(masked, axis=0, keepdims=True)
+        weights = jnp.exp2((masked - peak) * fold)
+        total = jnp.sum(weights, axis=0, keepdims=True)
+        values = jnp.concatenate(
+            [flipped[b * rows : (b + 1) * rows] for b in range(prior + 1)], axis=1
+        )
+        mixed = jnp.dot(values, weights.astype(jnp.bfloat16), preferred_element_type=jnp.float32)
+        mixed = mixed * (1.0 / total)
+        return jnp.concatenate(
+            [mixed[:, h * rows : (h + 1) * rows].T for h in range(SHARE)], axis=1
+        ).astype(jnp.bfloat16)
+
+    def encode(g):
+        first = pl.multiple_of(g * columns, columns)
+        encoded = attend(q_buf[:, pl.ds(first, columns)], kv[g, 0], kv[g, 1], bias)
+        enc_ref[:, pl.ds(first, columns)] = encoded
         picked = jnp.dot(choose, encoded, preferred_element_type=jnp.float32)
         squared = picked * picked
         for h in range(SHARE):
@@ -273,7 +276,7 @@
 
         @pl.when((g >= 0) & (g < KV_HEADS))
         def _():
-            attend(g)
+            encode(g)
             each_share(g, lambda copy: copy.start())
 
             @pl.when(g // per == tp)
@@ -376,7 +379,7 @@
             pltpu.VMEM((rows, D), bf16),
             pltpu.VMEM((width, cols), bf16),
             pltpu.VMEM((KV_HEADS, 2, span, HEAD_DIM), bf16),
-            pltpu.VMEM((rows, span), jnp.float32),
+            pltpu.VMEM((span, rows), jnp.float32),
             pltpu.VMEM((picks, HEAD_DIM), jnp.float32),
             pltpu.VMEM((KV_HEADS, 2 * picks, half), bf16),
             pltpu.VMEM((per, n, 2 * picks, half), bf16),

time: 65.9 us -> 65.9 us (level)
  no operation moved by 1% of the time
where the time goes in v5:
time: 65.9 us; the launch traced here: 65.2 us
  Pallas kernels  64.6 us (98%)
    pallas_call x1, Pallas kernels, on_device(): pl.pallas_call(functools.partial(kernel, n_tp, n_seq, prior), out_shape=(...  62.5 us
    pallas_call x1, Pallas kernels, on_device(): pl.pallas_call(hand_over, out_shape=tuple((jax.ShapeDtypeStruct(r.shape,...  2.05 us

profile of v5, /device:TPU:0, one launch (start us, length us, event | category | flops | bytes accessed | tf_op | source)
XLA Modules:
  0.0 65.2 jit_solution(7366218994727569830)
XLA Ops:
  0.6 62.5 %shard_map.77 = (bf16[128,4096]{1,0:T(8,128)(2,1)}, bf16[32,1536]{1,0:T(8,128)(2,1)}) custom-call(bf16[128,4096]{1,0:T(8,128)(2,1)} %q_hbm.1, bf16[128,1024]{1,0:T(8,128)(2,1)} %k_ref.1, bf16[128,1024]{1,0:T(8,128)(2,1)} %v_ref.1, s32[8]{0:T(128)} %pos_ref.1, f32[1,4096]{1,0:T(1,128)} %bitcast.1, bf16[1024,1536]{1,0:T(8,128)(2,1)} %w_hbm.1), custom_call_target="tpu_custom_call" | custom-call | flops 1744830464 | bytes 6291456 | tf_op jit(solution)/shard_map/pallas_call | solution.py:368
  63.2 2.1 %shard_map.78 = (bf16[128,4096]{1,0:T(8,128)(2,1)}, bf16[32,1536]{1,0:T(8,128)(2,1)}) custom-call(bf16[128,4096]{1,0:T(8,128)(2,1)} %get-tuple-element.4.enc_from, bf16[32,1536]{1,0:T(8,128)(2,1)} %get-tuple-element.5.sum_from), custom_call_target="tpu_custom_call" | custom-call | tf_op jit(solution)/shard_map/pallas_call | solution.py:409

commit v6 on v4

--- a/solution.py
+++ b/solution.py
@@ -50,6 +50,7 @@
     me = tp * n_seq + seq
     n = n_tp * n_seq
     rows = k_ref.shape[0]
+    assert rows == HEAD_DIM
     span = (prior + 1) * rows
     picks = pos_ref.shape[0]
     per = KV_HEADS // n_tp
@@ -87,7 +88,7 @@
 
     for g in range(KV_HEADS):
         kv[g, 0, (prior + 1) * rows : (prior + 2) * rows, :] = k_ref[:, g * HEAD_DIM : (g + 1) * HEAD_DIM]
-        kv[g, 1, (prior + 1) * rows : (prior + 2) * rows, :] = v_ref[:, g * HEAD_DIM : (g + 1) * HEAD_DIM]
+        kv[g, 1, (prior + 1) * rows : (prior + 2) * rows, :] = v_ref[:, g * HEAD_DIM : (g + 1) * HEAD_DIM].T
     for k in range(1, prior + 1):
 
         @pl.when(me < k)
@@ -97,8 +98,8 @@
                 (KV_HEADS, 2, rows, HEAD_DIM), jnp.bfloat16
             )
 
-    row = lax.broadcasted_iota(jnp.int32, (rows, span), 0)
-    col = lax.broadcasted_iota(jnp.int32, (rows, span), 1) - prior * rows
+    row = lax.broadcasted_iota(jnp.int32, (span, rows), 1)
+    col = lax.broadcasted_iota(jnp.int32, (span, rows), 0) - prior * rows
     band = (col <= row) & (col > row - WINDOW)
     bias[...] = jnp.where(band & (col + me * rows >= 0), 0.0, -jnp.inf).astype(jnp.float32)
     help_seen = band & (col + (me + outward) * rows >= 0)
@@ -233,24 +234,25 @@
 
     fold = math.log2(math.e) / HEAD_DIM**0.5
 
-    def attend(q_all, keys, values, bias):
+    def attend(q_all, keys, flipped, bias):
         q_rows = jnp.concatenate(
             [q_all[:, h * HEAD_DIM : (h + 1) * HEAD_DIM] for h in range(SHARE)], axis=0
         )
         scores = lax.dot_general(
-            q_rows, keys, (((1,), (1,)), ((), ())), preferred_element_type=jnp.float32
-        )
-        outs = []
-        for h in range(SHARE):
-            masked = scores[h * rows : (h + 1) * rows] + bias[...]
-            peak = jnp.max(masked, axis=1, keepdims=True)
-            weights = jnp.exp2((masked - peak) * fold)
-            total = jnp.sum(weights, axis=1, keepdims=True)
-            mixed = jnp.dot(
-                weights.astype(jnp.bfloat16), values, preferred_element_type=jnp.float32
-            )
-            outs.append((mixed / total).astype(jnp.bfloat16))
-        return jnp.concatenate(outs, axis=1)
+            keys, q_rows, (((1,), (1,)), ((), ())), preferred_element_type=jnp.float32
+        )
+        masked = scores + jnp.concatenate([bias[...]] * SHARE, axis=1)
+        peak = jnp.max(masked, axis=0, keepdims=True)
+        weights = jnp.exp2((masked - peak) * fold)
+        total = jnp.sum(weights, axis=0, keepdims=True)
+        values = jnp.concatenate(
+            [flipped[b * rows : (b + 1) * rows] for b in range(prior + 1)], axis=1
+        )
+        mixed = jnp.dot(values, weights.astype(jnp.bfloat16), preferred_element_type=jnp.float32)
+        mixed = mixed * (1.0 / total)
+        return jnp.concatenate(
+            [mixed[:, h * rows : (h + 1) * rows].T for h in range(SHARE)], axis=1
+        ).astype(jnp.bfloat16)
 
     def encode(g):
         first = pl.multiple_of(g * columns, columns)
@@ -480,8 +482,8 @@
             pltpu.VMEM((rows, D), bf16),
             pltpu.VMEM((width, cols), bf16),
             pltpu.VMEM((KV_HEADS, 2, (prior + 3) * rows, HEAD_DIM), bf16),
-            pltpu.VMEM((rows, span), jnp.float32),
-            pltpu.VMEM((rows, span), jnp.float32),
+            pltpu.VMEM((span, rows), jnp.float32),
+            pltpu.VMEM((span, rows), jnp.float32),
             pltpu.VMEM((picks, HEAD_DIM), jnp.float32),
             pltpu.VMEM((KV_HEADS, 2 * picks, half), bf16),
             pltpu.VMEM((per, n, 2 * picks, half), bf16),

time: 78.8 us -> 78.7 us (level)
  no operation moved by 1% of the time
where the time goes in v6:
time: 78.7 us; the launch traced here: 78 us
  Pallas kernels  77.4 us (98%)
    pallas_call x1, Pallas kernels, on_device(): pl.pallas_call(functools.partial(kernel, n_tp, n_seq, prior), out_shape=(...  75.3 us
    pallas_call x1, Pallas kernels, on_device(): pl.pallas_call(hand_over, out_shape=tuple((jax.ShapeDtypeStruct(r.shape,...  2.05 us

profile of v6, /device:TPU:0, one launch (start us, length us, event | category | flops | bytes accessed | tf_op | source)
XLA Modules:
  0.0 78.0 jit_solution(17896137805061346923)
XLA Ops:
  0.6 75.3 %shard_map.77 = (bf16[128,4096]{1,0:T(8,128)(2,1)}, bf16[32,1536]{1,0:T(8,128)(2,1)}) custom-call(bf16[128,4096]{1,0:T(8,128)(2,1)} %q_hbm.1, bf16[128,1024]{1,0:T(8,128)(2,1)} %k_ref.1, bf16[128,1024]{1,0:T(8,128)(2,1)} %v_ref.1, s32[8]{0:T(128)} %pos_ref.1, f32[1,4096]{1,0:T(1,128)} %bitcast.1, bf16[1024,1536]{1,0:T(8,128)(2,1)} %w_hbm.1), custom_call_target="tpu_custom_call" | custom-call | flops 1744830464 | bytes 6291456 | tf_op jit(solution)/shard_map/pallas_call | solution.py:471
  76.0 2.1 %shard_map.78 = (bf16[128,4096]{1,0:T(8,128)(2,1)}, bf16[32,1536]{1,0:T(8,128)(2,1)}) custom-call(bf16[128,4096]{1,0:T(8,128)(2,1)} %get-tuple-element.4.enc_from, bf16[32,1536]{1,0:T(8,128)(2,1)} %get-tuple-element.5.sum_from), custom_call_target="tpu_custom_call" | custom-call | tf_op jit(solution)/shard_map/pallas_call | solution.py:520

commit v7 on v5

--- a/solution.py
+++ b/solution.py
@@ -15,7 +15,9 @@
 WINDOW = 512
 SHARE = HEADS // KV_HEADS
 MESH = pl.DeviceIdType.MESH
-AHEAD = 3
+AHEAD = 4
+LEAD = 2
+LAG = 2
 PIECES = 4
 
 
@@ -102,58 +104,48 @@
     def slot(c, k):
         return kv.at[c, :, pl.ds((prior - k) * rows, rows), :]
 
-    def send(c, k, lands, way, target):
+    def send(c, k, lands, target, way):
         return pltpu.make_async_remote_copy(
             src_ref=slot(c, k),
             dst_ref=slot(c, lands),
-            send_sem=kv_send.at[way, k, c],
+            send_sem=kv_send.at[way, c],
             recv_sem=kv_recv.at[lands, c],
             device_id=target,
             device_id_type=MESH,
         )
 
-    def up(c, k):
-        return send(c, k, k + 1, 0, {"tp": tp, "seq": seq + 1})
-
-    def down(c, k):
-        return send(c, k, k - 1, 1, {"tp": tp, "seq": seq - 1})
-
-    def far(c):
-        return send(c, 0, prior, 1, {"tp": tp + 1, "seq": seq + prior - n_seq})
-
-    has_up = seq + 1 < n_seq
-    has_far = (seq + prior >= n_seq) & (tp + 1 < n_tp)
+    def each_own(c, act):
+        for k in range(1, prior + 1):
+            direct = me + k < n
+            if k == 1:
+                direct = direct & (seq + 1 < n_seq)
+            if k == 3:
+                direct = direct & (seq + 3 >= n_seq)
+
+            @pl.when(direct)
+            def _():
+                act(send(c, 0, k, device(me + k), k))
+
+    def each_forward(c, act):
+        @pl.when((seq >= 2) & (seq + 1 < n_seq))
+        def _():
+            act(send(c, 2, 3, device(me + 1), 0))
+
+        @pl.when((seq == 1) & (tp > 0))
+        def _():
+            act(send(c, 2, 1, device(me - 1), 0))
+
+    def arrive(c, k):
+        @pl.when(me >= k)
+        def _():
+            send(c, 0, k, device(me), k).wait_recv()
 
     def own(c):
-        @pl.when(has_up)
-        def _():
-            up(c, 0).start()
-
-        @pl.when(has_far)
-        def _():
-            far(c).start()
-
-    def from_below(c, k):
-        @pl.when(seq >= k)
-        def _():
-            up(c, k - 1).wait_recv()
-
-            if k < prior:
-
-                @pl.when(has_up)
-                def _():
-                    up(c, k).start()
-
-    def from_before(c, k):
-        @pl.when((seq < k) & (tp > 0))
-        def _():
-            send(c, 0, k, 1, {"tp": tp, "seq": seq}).wait_recv()
-
-            if k >= 2:
-
-                @pl.when(seq >= 1)
-                def _():
-                    down(c, k).start()
+        each_own(c, lambda copy: copy.start())
+
+    def forward(c):
+        arrive(c, 2)
+        each_forward(c, lambda copy: copy.start())
 
     fold = math.log2(math.e) / HEAD_DIM**0.5
 
@@ -255,27 +247,26 @@
     pl.semaphore_wait(barrier, n - 1)
     for c in range(AHEAD):
         own(c)
+    for c in range(LEAD):
+        forward(c)
     q_copy.wait()
     w_copy.wait()
 
-    @pl.loop(0, KV_HEADS + prior)
-    def _(t):
-        @pl.when(t + AHEAD < KV_HEADS)
-        def _():
-            own(t + AHEAD)
-
-        for depth in range(1, prior + 1):
-            c = t - (depth - 1)
-
-            @pl.when((c >= 0) & (c < KV_HEADS))
-            def _():
-                from_below(c, depth)
-                from_before(c, prior + 1 - depth)
-
-        g = t - (prior - 1)
-
-        @pl.when((g >= 0) & (g < KV_HEADS))
-        def _():
+    @pl.loop(0, KV_HEADS + LAG)
+    def _(g):
+        @pl.when(g + AHEAD < KV_HEADS)
+        def _():
+            own(g + AHEAD)
+
+        @pl.when(g + LEAD < KV_HEADS)
+        def _():
+            forward(g + LEAD)
+
+        @pl.when(g < KV_HEADS)
+        def _():
+            for k in range(1, prior + 1):
+                if k != 2:
+                    arrive(g, k)
             encode(g)
             each_share(g, lambda copy: copy.start())
 
@@ -290,9 +281,9 @@
             for step in range(1, n_seq):
                 scale_to(step).start()
 
-        @pl.when((g >= 1) & ((g - 1) // per == tp))
-        def _():
-            project(g - 1)
+        @pl.when((g >= LAG) & ((g - LAG) // per == tp))
+        def _():
+            project(g - LAG)
 
     total = part[tp].astype(jnp.float32)
     for step in range(1, n_tp):
@@ -330,25 +321,8 @@
 
     @pl.loop(0, KV_HEADS)
     def _(c):
-        @pl.when(has_up)
-        def _():
-            up(c, 0).wait_send()
-
-        @pl.when(has_far)
-        def _():
-            far(c).wait_send()
-
-        for k in range(1, prior):
-
-            @pl.when((seq >= k) & has_up)
-            def _():
-                up(c, k).wait_send()
-
-        for k in range(2, prior + 1):
-
-            @pl.when((seq < k) & (tp > 0) & (seq >= 1))
-            def _():
-                down(c, k).wait_send()
+        each_own(c, lambda copy: copy.wait_send())
+        each_forward(c, lambda copy: copy.wait_send())
 
 
 def on_device(n_tp, n_seq, queries, keys, values, mem_pos, norm_gain, summary_weight):
@@ -388,7 +362,7 @@
             pltpu.VMEM((n_tp, n_seq * picks, cols), bf16),
             pltpu.VMEM((n_seq, picks, HEAD_DIM), jnp.float32),
             dma((2,)),
-            dma((2, prior + 1, KV_HEADS)),
+            dma((prior + 1, KV_HEADS)),
             dma((prior + 1, KV_HEADS)),
             dma((KV_HEADS, n_seq)),
             dma((per, n)),

time: 65.9 us -> 64.2 us (0.974)
  Pallas kernels: 64.6 us -> 62.8 us
    pallas_call x1, Pallas kernels: 62.5 us -> 60.8 us  [on_device(): pl.pallas_call(functools.partial(kernel, n_tp, n_seq, prior), out_shape=(...]
where the time goes in v7:
time: 64.2 us; the launch traced here: 63.5 us
  Pallas kernels  62.8 us (98%)
    pallas_call x1, Pallas kernels, on_device(): pl.pallas_call(functools.partial(kernel, n_tp, n_seq, prior), out_shape=(...  60.8 us
    pallas_call x1, Pallas kernels, on_device(): pl.pallas_call(hand_over, out_shape=tuple((jax.ShapeDtypeStruct(r.shape,...  2.05 us

profile of v7, /device:TPU:0, one launch (start us, length us, event | category | flops | bytes accessed | tf_op | source)
XLA Modules:
  0.0 63.5 jit_solution(1480243092779992166)
XLA Ops:
  0.6 60.8 %shard_map.77 = (bf16[128,4096]{1,0:T(8,128)(2,1)}, bf16[32,1536]{1,0:T(8,128)(2,1)}) custom-call(bf16[128,4096]{1,0:T(8,128)(2,1)} %q_hbm.1, bf16[128,1024]{1,0:T(8,128)(2,1)} %k_ref.1, bf16[128,1024]{1,0:T(8,128)(2,1)} %v_ref.1, s32[8]{0:T(128)} %pos_ref.1, f32[1,4096]{1,0:T(1,128)} %bitcast.1, bf16[1024,1536]{1,0:T(8,128)(2,1)} %w_hbm.1), custom_call_target="tpu_custom_call" | custom-call | flops 1744830464 | bytes 6291456 | tf_op jit(solution)/shard_map/pallas_call | solution.py:342
  61.4 2.1 %shard_map.78 = (bf16[128,4096]{1,0:T(8,128)(2,1)}, bf16[32,1536]{1,0:T(8,128)(2,1)}) custom-call(bf16[128,4096]{1,0:T(8,128)(2,1)} %get-tuple-element.4.enc_from, bf16[32,1536]{1,0:T(8,128)(2,1)} %get-tuple-element.5.sum_from), custom_call_target="tpu_custom_call" | custom-call | tf_op jit(solution)/shard_map/pallas_call | solution.py:383

commit v8 on v7

--- a/solution.py
+++ b/solution.py
@@ -15,9 +15,9 @@
 WINDOW = 512
 SHARE = HEADS // KV_HEADS
 MESH = pl.DeviceIdType.MESH
-AHEAD = 4
-LEAD = 2
-LAG = 2
+AHEAD = 2
+LEAD = 1
+LAG = 1
 PIECES = 4
 
 
@@ -42,7 +42,7 @@
     n_tp, n_seq, prior,
     q_hbm, k_ref, v_ref, pos_ref, gain_ref, w_hbm,
     enc_ref, sum_ref,
-    q_buf, w_buf, kv, bias, squares, mine, mem, sums, part, red, scales,
+    q_buf, w_buf, kv, bias, squares, mine, mem, part, red, scales,
     local_sem, kv_send, kv_recv, mem_send, mem_recv, red_send, red_recv, scale_send, scale_recv,
 ):
     tp = lax.axis_index("tp")
@@ -55,11 +55,10 @@
     picks = pos_ref.shape[0]
     per = KV_HEADS // n_tp
     columns = SHARE * HEAD_DIM
-    half = columns // 2
+    chunks = KV_HEADS // per
     cols = sum_ref.shape[1]
     tile = 512 if cols % 512 == 0 else cols
     squares[...] = jnp.zeros_like(squares)
-    sums[...] = jnp.zeros_like(sums)
 
     def device(index):
         return {"tp": index // n_seq, "seq": index % n_seq}
@@ -102,7 +101,7 @@
     choose = jnp.where(pick_col == wanted, 1.0, 0.0).astype(jnp.bfloat16)
 
     def slot(c, k):
-        return kv.at[c, :, pl.ds((prior - k) * rows, rows), :]
+        return kv.at[pl.ds(c * per, per), :, pl.ds((prior - k) * rows, rows), :]
 
     def send(c, k, lands, target, way):
         return pltpu.make_async_remote_copy(
@@ -169,34 +168,37 @@
             [mixed[:, h * rows : (h + 1) * rows].T for h in range(SHARE)], axis=1
         ).astype(jnp.bfloat16)
 
-    def encode(g):
-        first = pl.multiple_of(g * columns, columns)
-        encoded = attend(q_buf[:, pl.ds(first, columns)], kv[g, 0], kv[g, 1], bias)
-        enc_ref[:, pl.ds(first, columns)] = encoded
-        picked = jnp.dot(choose, encoded, preferred_element_type=jnp.float32)
-        squared = picked * picked
-        for h in range(SHARE):
-            squares[...] += squared[:, h * HEAD_DIM : (h + 1) * HEAD_DIM]
-        gained = picked * gain_ref[:, pl.ds(first, columns)]
-        mine[g] = jnp.concatenate((gained[:, :half], gained[:, half:]), axis=0).astype(jnp.bfloat16)
-
-    def share(g, s, source):
+    def encode(c):
+        gained = []
+        for j in range(per):
+            g = c * per + j
+            first = pl.multiple_of(g * columns, columns)
+            encoded = attend(q_buf[:, pl.ds(first, columns)], kv[g, 0], kv[g, 1], bias)
+            enc_ref[:, pl.ds(first, columns)] = encoded
+            picked = jnp.dot(choose, encoded, preferred_element_type=jnp.float32)
+            squared = picked * picked
+            for h in range(SHARE):
+                squares[...] += squared[:, h * HEAD_DIM : (h + 1) * HEAD_DIM]
+            gained.append(picked * gain_ref[:, pl.ds(first, columns)])
+        mine[c] = jnp.concatenate(gained, axis=0).astype(jnp.bfloat16)
+
+    def share(c, s, source):
         return pltpu.make_async_remote_copy(
-            src_ref=mine.at[g],
-            dst_ref=mem.at[g % per, source],
-            send_sem=mem_send.at[g, s],
-            recv_sem=mem_recv.at[g % per, source],
-            device_id={"tp": g // per, "seq": s},
-            device_id_type=MESH,
-        )
-
-    def each_share(g, act):
+            src_ref=mine.at[c],
+            dst_ref=mem.at[source],
+            send_sem=mem_send.at[c, s],
+            recv_sem=mem_recv.at[source],
+            device_id={"tp": c, "seq": s},
+            device_id_type=MESH,
+        )
+
+    def each_share(c, act):
         for step in range(1, n_seq):
-            act(share(g, (seq + step) % n_seq, me))
-
-        @pl.when(g // per != tp)
-        def _():
-            act(share(g, seq, me))
+            act(share(c, (seq + step) % n_seq, me))
+
+        @pl.when(c != tp)
+        def _():
+            act(share(c, seq, me))
 
     def scale_to(step):
         return pltpu.make_async_remote_copy(
@@ -219,30 +221,26 @@
             device_id_type=MESH,
         )
 
-    def project(g):
-        place = g % per
-
+    def project():
         @pl.loop(1, n)
         def _(step):
             source = (me + step) % n
-            share(per * tp + place, seq, source).wait_recv()
-
-        gathered = mem[place].astype(jnp.float32)
-        left = gathered[:, :picks].reshape(n * picks, half)
-        right = gathered[:, picks:].reshape(n * picks, half)
-        memory = jnp.concatenate((left, right), axis=1).astype(jnp.bfloat16)
-        down_to = pl.multiple_of(place * columns, columns)
+            share(tp, seq, source).wait_recv()
+
+        gathered = mem[...].astype(jnp.float32)
+        memory = jnp.concatenate(
+            [
+                gathered[:, j * picks : (j + 1) * picks].reshape(n * picks, columns)
+                for j in range(per)
+            ],
+            axis=1,
+        ).astype(jnp.bfloat16)
         for j in range(cols // tile):
             where = slice(j * tile, (j + 1) * tile)
-            sums[:, where] += jnp.dot(
-                memory, w_buf[pl.ds(down_to, columns), where], preferred_element_type=jnp.float32
-            )
-
-        @pl.when(place == per - 1)
-        def _():
-            part[...] = sums[...].reshape(n_tp, n_seq * picks, cols).astype(jnp.bfloat16)
-            for step in range(1, n_tp):
-                reduce(step).start()
+            sums = jnp.dot(memory, w_buf[:, where], preferred_element_type=jnp.float32)
+            part[:, :, where] = sums.reshape(n_tp, n_seq * picks, tile).astype(jnp.bfloat16)
+        for step in range(1, n_tp):
+            reduce(step).start()
 
     pl.semaphore_wait(barrier, n - 1)
     for c in range(AHEAD):
@@ -252,17 +250,17 @@
     q_copy.wait()
     w_copy.wait()
 
-    @pl.loop(0, KV_HEADS + LAG)
+    @pl.loop(0, chunks + LAG)
     def _(g):
-        @pl.when(g + AHEAD < KV_HEADS)
+        @pl.when(g + AHEAD < chunks)
         def _():
             own(g + AHEAD)
 
-        @pl.when(g + LEAD < KV_HEADS)
+        @pl.when(g + LEAD < chunks)
         def _():
             forward(g + LEAD)
 
-        @pl.when(g < KV_HEADS)
+        @pl.when(g < chunks)
         def _():
             for k in range(1, prior + 1):
                 if k != 2:
@@ -270,20 +268,26 @@
             encode(g)
             each_share(g, lambda copy: copy.start())
 
-            @pl.when(g // per == tp)
+            @pl.when(g == tp)
             def _():
-                mem[g % per, me] = mine[g]
-
-        @pl.when(g == KV_HEADS - 1)
+                mem[me] = mine[g]
+
+        @pl.when(g == chunks - 1)
         def _():
             meansq = jnp.sum(squares[...], axis=1, keepdims=True) / D
             scales[seq] = jnp.broadcast_to(lax.rsqrt(meansq + 1e-05), scales.shape[1:])
             for step in range(1, n_seq):
                 scale_to(step).start()
 
-        @pl.when((g >= LAG) & ((g - LAG) // per == tp))
-        def _():
-            project(g - LAG)
+        @pl.when(g - LAG == tp)
+        def _():
+            project()
+
+    @pl.loop(0, chunks)
+    def _(c):
+        each_share(c, lambda copy: copy.wait_send())
+        each_own(c, lambda copy: copy.wait_send())
+        each_forward(c, lambda copy: copy.wait_send())
 
     total = part[tp].astype(jnp.float32)
     for step in range(1, n_tp):
@@ -315,15 +319,6 @@
     for step in range(1, n_seq):
         scale_to(step).wait_send()
 
-    @pl.loop(0, KV_HEADS)
-    def _(g):
-        each_share(g, lambda copy: copy.wait_send())
-
-    @pl.loop(0, KV_HEADS)
-    def _(c):
-        each_own(c, lambda copy: copy.wait_send())
-        each_forward(c, lambda copy: copy.wait_send())
-
 
 def on_device(n_tp, n_seq, queries, keys, values, mem_pos, norm_gain, summary_weight):
     rows = queries.shape[0]
@@ -333,7 +328,8 @@
     width = summary_weight.shape[0]
     cols = summary_weight.shape[1]
     per = KV_HEADS // n_tp
-    half = width // per // 2
+    chunks = KV_HEADS // per
+    columns = width // per
     vmem = pl.BlockSpec(memory_space=pltpu.VMEM)
     anywhere = pl.BlockSpec(memory_space=pl.ANY)
     bf16 = jnp.bfloat16
@@ -355,17 +351,16 @@
             pltpu.VMEM((KV_HEADS, 2, span, HEAD_DIM), bf16),
             pltpu.VMEM((span, rows), jnp.float32),
             pltpu.VMEM((picks, HEAD_DIM), jnp.float32),
-            pltpu.VMEM((KV_HEADS, 2 * picks, half), bf16),
-            pltpu.VMEM((per, n, 2 * picks, half), bf16),
-            pltpu.VMEM((n * picks, cols), jnp.float32),
+            pltpu.VMEM((chunks, per * picks, columns), bf16),
+            pltpu.VMEM((n, per * picks, columns), bf16),
             pltpu.VMEM((n_tp, n_seq * picks, cols), bf16),
             pltpu.VMEM((n_tp, n_seq * picks, cols), bf16),
             pltpu.VMEM((n_seq, picks, HEAD_DIM), jnp.float32),
             dma((2,)),
-            dma((prior + 1, KV_HEADS)),
-            dma((prior + 1, KV_HEADS)),
-            dma((KV_HEADS, n_seq)),
-            dma((per, n)),
+            dma((prior + 1, chunks)),
+            dma((prior + 1, chunks)),
+            dma((chunks, n_seq)),
+            dma((n,)),
             dma((n_tp,)),
             dma((n_tp,)),
             dma((n_seq,)),

time: 64.2 us -> 64.1 us (level)
  no operation moved by 1% of the time
where the time goes in v8:
time: 64.1 us; the launch traced here: 63.2 us
  Pallas kernels  62.6 us (98%)
    pallas_call x1, Pallas kernels, on_device(): pl.pallas_call(functools.partial(kernel, n_tp, n_seq, prior), out_shape=(...  60.6 us
    pallas_call x1, Pallas kernels, on_device(): pl.pallas_call(hand_over, out_shape=tuple((jax.ShapeDtypeStruct(r.shape,...  2.05 us

profile of v8, /device:TPU:0, one launch (start us, length us, event | category | flops | bytes accessed | tf_op | source)
XLA Modules:
  0.0 63.2 jit_solution(398807224370607570)
XLA Ops:
  0.6 60.6 %shard_map.77 = (bf16[128,4096]{1,0:T(8,128)(2,1)}, bf16[32,1536]{1,0:T(8,128)(2,1)}) custom-call(bf16[128,4096]{1,0:T(8,128)(2,1)} %q_hbm.1, bf16[128,1024]{1,0:T(8,128)(2,1)} %k_ref.1, bf16[128,1024]{1,0:T(8,128)(2,1)} %v_ref.1, s32[8]{0:T(128)} %pos_ref.1, f32[1,4096]{1,0:T(1,128)} %bitcast.1, bf16[1024,1536]{1,0:T(8,128)(2,1)} %w_hbm.1), custom_call_target="tpu_custom_call" | custom-call | flops 1744830464 | bytes 6291456 | tf_op jit(solution)/shard_map/pallas_call | solution.py:338
  61.2 2.1 %shard_map.78 = (bf16[128,4096]{1,0:T(8,128)(2,1)}, bf16[32,1536]{1,0:T(8,128)(2,1)}) custom-call(bf16[128,4096]{1,0:T(8,128)(2,1)} %get-tuple-element.4.enc_from, bf16[32,1536]{1,0:T(8,128)(2,1)} %get-tuple-element.5.sum_from), custom_call_target="tpu_custom_call" | custom-call | tf_op jit(solution)/shard_map/pallas_call | solution.py:378

commit v9 on v8

--- a/solution.py
+++ b/solution.py
@@ -42,7 +42,7 @@
     n_tp, n_seq, prior,
     q_hbm, k_ref, v_ref, pos_ref, gain_ref, w_hbm,
     enc_ref, sum_ref,
-    q_buf, w_buf, kv, bias, squares, mine, mem, part, red, scales,
+    q_buf, w_buf, kv, bias, squares, mine, mem, part, red, scales, enc_buf, enc_sem,
     local_sem, kv_send, kv_recv, mem_send, mem_recv, red_send, red_recv, scale_send, scale_recv,
 ):
     tp = lax.axis_index("tp")
@@ -174,13 +174,17 @@
             g = c * per + j
             first = pl.multiple_of(g * columns, columns)
             encoded = attend(q_buf[:, pl.ds(first, columns)], kv[g, 0], kv[g, 1], bias)
-            enc_ref[:, pl.ds(first, columns)] = encoded
+            enc_buf[:, pl.ds(first, columns)] = encoded
             picked = jnp.dot(choose, encoded, preferred_element_type=jnp.float32)
             squared = picked * picked
             for h in range(SHARE):
                 squares[...] += squared[:, h * HEAD_DIM : (h + 1) * HEAD_DIM]
             gained.append(picked * gain_ref[:, pl.ds(first, columns)])
         mine[c] = jnp.concatenate(gained, axis=0).astype(jnp.bfloat16)
+
+    def write(c):
+        where = pl.ds(pl.multiple_of(c * per * columns, columns), per * columns)
+        return pltpu.make_async_copy(enc_buf.at[:, where], enc_ref.at[:, where], enc_sem.at[c])
 
     def share(c, s, source):
         return pltpu.make_async_remote_copy(
@@ -210,13 +214,13 @@
             device_id_type=MESH,
         )
 
-    def reduce(step):
+    def reduce(step, j):
         other = (tp + step) % n_tp
         return pltpu.make_async_remote_copy(
-            src_ref=part.at[other],
-            dst_ref=red.at[tp],
-            send_sem=red_send.at[step],
-            recv_sem=red_recv.at[tp],
+            src_ref=part.at[j, other],
+            dst_ref=red.at[j, tp],
+            send_sem=red_send.at[step, j],
+            recv_sem=red_recv.at[tp, j],
             device_id={"tp": other, "seq": seq},
             device_id_type=MESH,
         )
@@ -238,9 +242,9 @@
         for j in range(cols // tile):
             where = slice(j * tile, (j + 1) * tile)
             sums = jnp.dot(memory, w_buf[:, where], preferred_element_type=jnp.float32)
-            part[:, :, where] = sums.reshape(n_tp, n_seq * picks, tile).astype(jnp.bfloat16)
-        for step in range(1, n_tp):
-            reduce(step).start()
+            part[j] = sums.reshape(n_tp, n_seq * picks, tile).astype(jnp.bfloat16)
+            for step in range(1, n_tp):
+                reduce(step, j).start()
 
     pl.semaphore_wait(barrier, n - 1)
     for c in range(AHEAD):
@@ -267,6 +271,7 @@
                     arrive(g, k)
             encode(g)
             each_share(g, lambda copy: copy.start())
+            write(g).start()
 
             @pl.when(g == tp)
             def _():
@@ -285,22 +290,11 @@
 
     @pl.loop(0, chunks)
     def _(c):
+        write(c).wait()
         each_share(c, lambda copy: copy.wait_send())
         each_own(c, lambda copy: copy.wait_send())
         each_forward(c, lambda copy: copy.wait_send())
 
-    total = part[tp].astype(jnp.float32)
-    for step in range(1, n_tp):
-        source = (tp + step) % n_tp
-        pltpu.make_async_remote_copy(
-            src_ref=part.at[0],
-            dst_ref=red.at[source],
-            send_sem=red_send.at[step],
-            recv_sem=red_recv.at[source],
-            device_id={"tp": source, "seq": seq},
-            device_id_type=MESH,
-        ).wait_recv()
-        total = total + red[source].astype(jnp.float32)
     for step in range(1, n_seq):
         source = (seq + step) % n_seq
         pltpu.make_async_remote_copy(
@@ -312,10 +306,25 @@
             device_id_type=MESH,
         ).wait_recv()
     factor = scales[...].reshape(n_seq * picks, HEAD_DIM)[:, :1]
-    sum_ref[...] = (total * factor).astype(jnp.bfloat16)
-
-    for step in range(1, n_tp):
-        reduce(step).wait_send()
+
+    for j in range(cols // tile):
+        total = part[j, tp].astype(jnp.float32)
+        for step in range(1, n_tp):
+            source = (tp + step) % n_tp
+            pltpu.make_async_remote_copy(
+                src_ref=part.at[j, 0],
+                dst_ref=red.at[j, source],
+                send_sem=red_send.at[step, j],
+                recv_sem=red_recv.at[source, j],
+                device_id={"tp": source, "seq": seq},
+                device_id_type=MESH,
+            ).wait_recv()
+            total = total + red[j, source].astype(jnp.float32)
+        sum_ref[:, j * tile : (j + 1) * tile] = (total * factor).astype(jnp.bfloat16)
+
+    for j in range(cols // tile):
+        for step in range(1, n_tp):
+            reduce(step, j).wait_send()
     for step in range(1, n_seq):
         scale_to(step).wait_send()
 
@@ -330,6 +339,7 @@
     per = KV_HEADS // n_tp
     chunks = KV_HEADS // per
     columns = width // per
+    tiles = cols // 512 if cols % 512 == 0 else 1
     vmem = pl.BlockSpec(memory_space=pltpu.VMEM)
     anywhere = pl.BlockSpec(memory_space=pl.ANY)
     bf16 = jnp.bfloat16
@@ -344,7 +354,7 @@
         in_specs=[
             anywhere, vmem, vmem, pl.BlockSpec(memory_space=pltpu.SMEM), vmem, anywhere,
         ],
-        out_specs=(vmem, vmem),
+        out_specs=(anywhere, vmem),
         scratch_shapes=[
             pltpu.VMEM((rows, D), bf16),
             pltpu.VMEM((width, cols), bf16),
@@ -353,16 +363,18 @@
             pltpu.VMEM((picks, HEAD_DIM), jnp.float32),
             pltpu.VMEM((chunks, per * picks, columns), bf16),
             pltpu.VMEM((n, per * picks, columns), bf16),
-            pltpu.VMEM((n_tp, n_seq * picks, cols), bf16),
-            pltpu.VMEM((n_tp, n_seq * picks, cols), bf16),
+            pltpu.VMEM((tiles, n_tp, n_seq * picks, cols // tiles), bf16),
+            pltpu.VMEM((tiles, n_tp, n_seq * picks, cols // tiles), bf16),
             pltpu.VMEM((n_seq, picks, HEAD_DIM), jnp.float32),
+            pltpu.VMEM((rows, D), bf16),
+            dma((chunks,)),
             dma((2,)),
             dma((prior + 1, chunks)),
             dma((prior + 1, chunks)),
             dma((chunks, n_seq)),
             dma((n,)),
-            dma((n_tp,)),
-            dma((n_tp,)),
+            dma((n_tp, tiles)),
+            dma((n_tp, tiles)),
             dma((n_seq,)),
             dma((n_seq,)),
         ],

time: 64.1 us -> 63.8 us (level)
  no operation moved by 1% of the time
where the time goes in v9:
time: 63.8 us; the launch traced here: 63.6 us
  Pallas kernels  62.9 us (99%)
  between operations  0.64 us (1%)
    pallas_call x1, Pallas kernels, on_device(): pl.pallas_call(functools.partial(kernel, n_tp, n_seq, prior), out_shape=(...  60.9 us
    pallas_call x1, Pallas kernels, on_device(): pl.pallas_call(hand_over, out_shape=tuple((jax.ShapeDtypeStruct(r.shape,...  2.05 us

profile of v9, /device:TPU:0, one launch (start us, length us, event | category | flops | bytes accessed | tf_op | source)
XLA Modules:
  0.0 63.6 jit_solution(8314912944379456838)
XLA Ops:
  0.6 60.9 %shard_map.77 = (bf16[128,4096]{1,0:T(8,128)(2,1)}, bf16[32,1536]{1,0:T(8,128)(2,1)}) custom-call(bf16[128,4096]{1,0:T(8,128)(2,1)} %q_hbm.1, bf16[128,1024]{1,0:T(8,128)(2,1)} %k_ref.1, bf16[128,1024]{1,0:T(8,128)(2,1)} %v_ref.1, s32[8]{0:T(128)} %pos_ref.1, f32[1,4096]{1,0:T(1,128)} %bitcast.1, bf16[1024,1536]{1,0:T(8,128)(2,1)} %w_hbm.1), custom_call_target="tpu_custom_call" | custom-call | flops 1744830464 | bytes 6291456 | tf_op jit(solution)/shard_map/pallas_call | solution.py:348
  61.5 2.1 %shard_map.78 = (bf16[128,4096]{1,0:T(8,128)(2,1)}, bf16[32,1536]{1,0:T(8,128)(2,1)}) custom-call(bf16[128,4096]{1,0:T(8,128)(2,1)} %get-tuple-element.4.enc_from, bf16[32,1536]{1,0:T(8,128)(2,1)} %get-tuple-element.5.sum_from), custom_call_target="tpu_custom_call" | custom-call | tf_op jit(solution)/shard_map/pallas_call | solution.py:390

commit v10 on v9

--- a/solution.py
+++ b/solution.py
@@ -40,9 +40,9 @@
 
 def kernel(
     n_tp, n_seq, prior,
-    q_hbm, k_ref, v_ref, pos_ref, gain_ref, w_hbm,
+    q_hbm, k_hbm, v_hbm, pos_ref, gain_ref, w_hbm,
     enc_ref, sum_ref,
-    q_buf, w_buf, kv, bias, squares, mine, mem, part, red, scales, enc_buf, enc_sem,
+    q_buf, k_ref, v_ref, w_buf, kv, bias, squares, mine, mem, part, red, scales, enc_buf, enc_sem,
     local_sem, kv_send, kv_recv, mem_send, mem_recv, red_send, red_recv, scale_send, scale_recv,
 ):
     tp = lax.axis_index("tp")
@@ -63,11 +63,6 @@
     def device(index):
         return {"tp": index // n_seq, "seq": index % n_seq}
 
-    q_copy = pltpu.make_async_copy(q_hbm, q_buf, local_sem.at[0])
-    w_copy = pltpu.make_async_copy(w_hbm, w_buf, local_sem.at[1])
-    q_copy.start()
-    w_copy.start()
-
     barrier = pltpu.get_barrier_semaphore()
 
     @pl.loop(1, n)
@@ -76,6 +71,14 @@
             barrier, inc=1, device_id=device((me + step) % n), device_id_type=MESH
         )
 
+    k_copy = pltpu.make_async_copy(k_hbm, k_ref, local_sem.at[2])
+    v_copy = pltpu.make_async_copy(v_hbm, v_ref, local_sem.at[3])
+    q_copy = pltpu.make_async_copy(q_hbm, q_buf, local_sem.at[0])
+    w_copy = pltpu.make_async_copy(w_hbm, w_buf, local_sem.at[1])
+    for copy in (k_copy, v_copy, q_copy, w_copy):
+        copy.start()
+    k_copy.wait()
+    v_copy.wait()
     for g in range(KV_HEADS):
         kv[g, 0, prior * rows :, :] = k_ref[:, g * HEAD_DIM : (g + 1) * HEAD_DIM]
         kv[g, 1, prior * rows :, :] = v_ref[:, g * HEAD_DIM : (g + 1) * HEAD_DIM].T
@@ -352,11 +355,13 @@
             jax.ShapeDtypeStruct((n_seq * picks, cols), bf16),
         ),
         in_specs=[
-            anywhere, vmem, vmem, pl.BlockSpec(memory_space=pltpu.SMEM), vmem, anywhere,
+            anywhere, anywhere, anywhere, pl.BlockSpec(memory_space=pltpu.SMEM), vmem, anywhere,
         ],
         out_specs=(anywhere, vmem),
         scratch_shapes=[
             pltpu.VMEM((rows, D), bf16),
+            pltpu.VMEM(keys.shape, bf16),
+            pltpu.VMEM(values.shape, bf16),
             pltpu.VMEM((width, cols), bf16),
             pltpu.VMEM((KV_HEADS, 2, span, HEAD_DIM), bf16),
             pltpu.VMEM((span, rows), jnp.float32),
@@ -368,7 +373,7 @@
             pltpu.VMEM((n_seq, picks, HEAD_DIM), jnp.float32),
             pltpu.VMEM((rows, D), bf16),
             dma((chunks,)),
-            dma((2,)),
+            dma((4,)),
             dma((prior + 1, chunks)),
             dma((prior + 1, chunks)),
             dma((chunks, n_seq)),

time: 63.8 us -> 63.5 us (level)
  no operation moved by 1% of the time
where the time goes in v10:
time: 63.5 us; the launch traced here: 63.3 us
  Pallas kernels  62.6 us (99%)
  between operations  0.64 us (1%)
    pallas_call x1, Pallas kernels, on_device(): pl.pallas_call(functools.partial(kernel, n_tp, n_seq, prior), out_shape=(...  60.6 us
    pallas_call x1, Pallas kernels, on_device(): pl.pallas_call(hand_over, out_shape=tuple((jax.ShapeDtypeStruct(r.shape,...  2.05 us

profile of v10, /device:TPU:0, one launch (start us, length us, event | category | flops | bytes accessed | tf_op | source)
XLA Modules:
  0.0 63.3 jit_solution(17883614033235036891)
XLA Ops:
  0.6 60.6 %shard_map.77 = (bf16[128,4096]{1,0:T(8,128)(2,1)}, bf16[32,1536]{1,0:T(8,128)(2,1)}) custom-call(bf16[128,4096]{1,0:T(8,128)(2,1)} %q_hbm.1, bf16[128,1024]{1,0:T(8,128)(2,1)} %k_hbm.1, bf16[128,1024]{1,0:T(8,128)(2,1)} %v_hbm.1, s32[8]{0:T(128)} %pos_ref.1, f32[1,4096]{1,0:T(1,128)} %bitcast.1, bf16[1024,1536]{1,0:T(8,128)(2,1)} %w_hbm.1), custom_call_target="tpu_custom_call" | custom-call | flops 1744830464 | bytes 6291456 | tf_op jit(solution)/shard_map/pallas_call | solution.py:351
  61.2 2.1 %shard_map.78 = (bf16[128,4096]{1,0:T(8,128)(2,1)}, bf16[32,1536]{1,0:T(8,128)(2,1)}) custom-call(bf16[128,4096]{1,0:T(8,128)(2,1)} %get-tuple-element.4.enc_from, bf16[32,1536]{1,0:T(8,128)(2,1)} %get-tuple-element.5.sum_from), custom_call_target="tpu_custom_call" | custom-call | tf_op jit(solution)/shard_map/pallas_call | solution.py:395
